TPU v7x, 32 devices: a whole 2x2x4 slice. The times are simulated.
32 devices in a mesh: row: 4 (over y, x), rep: 8 (over z, core).
Axes of the slice: x: 2, y: 2, z: 4, core: 2. Of those that a mesh axis runs over, the one named last changes fastest.
Arguments:
- features: bfloat16 [24576, 128], P(('row', 'rep')), may hold values from -6 to 6
- node_order: int32 [32, 768], P(('row', 'rep')), may hold values from 0 to 767, each once within a row
- weight: bfloat16 [128, 128], replicated, may hold values from -0.5 to 0.5
- tile_vals: bfloat16 [192, 8, 4, 128, 128], P('row', 'rep'), may hold values from -0.09375 to 0.09375
- tile_cols: int32 [192, 8, 4], P('row', 'rep'), may hold values from 0 to 23, as said below
- row_counts: int32 [192, 8], P('row', 'rep'), may hold values from 1 to 4
- cotangent: bfloat16 [24576, 128], P(('row', 'rep')), may hold values from -6 to 6
Outputs:
- hidden_out: bfloat16 [24576, 128], P(('row', 'rep'))
- feature_grad: bfloat16 [24576, 128], P(('row', 'rep'))
- weight_grad: float32 [128, 128], replicated
Inputs may be any that keep to these rules, and one draw needn't show every extreme that they name: `tile_cols`: within one tile-row and block-column the 4 slots name distinct tile-columns.
All inputs are finite; a program needn't handle non-finite values.
Results may differ from a plain program's by a relative error of at most 0.005.
Values may be sent and summed in bfloat16 or wider, within the bound.
A program may use at most 128 MiB of HBM per device.

v0:
```python
import math

import jax
import jax.numpy as jnp
from jax import lax
from jax.sharding import PartitionSpec as P


def aggregate(values, columns, counts, z_tiles, amount):
    tile_size = values.shape[2]
    slot_count = values.shape[1]
    picked = jnp.take(z_tiles, columns, axis=0)
    present = jnp.arange(slot_count)[None, :] < counts[:, None]
    masked = jnp.where(present[:, :, None, None], picked, jnp.zeros((), jnp.bfloat16))
    summed = jnp.einsum("rmab,rmbf->raf", values, masked, preferred_element_type=jnp.float32)
    return summed.reshape(amount * tile_size, summed.shape[2])


def shards(features, node_order, weight, tile_vals, tile_cols, row_counts, cotangent):
    tile_size = tile_vals.shape[3]
    slot_count = tile_vals.shape[2]
    slab_rows = features.shape[0]
    values = tile_vals[:, 0]
    columns = tile_cols[:, 0]
    counts = row_counts[:, 0]
    reordered = jnp.take(features, node_order[0], axis=0)
    projected = jnp.dot(reordered, weight, preferred_element_type=jnp.float32).astype(jnp.bfloat16)
    gathered_z = lax.all_gather(projected, "row", axis=0, tiled=True)
    z_tiles = gathered_z.reshape(-1, tile_size, gathered_z.shape[1])
    partial_sum = aggregate(values, columns, counts, z_tiles, values.shape[0])
    summed_rows = lax.psum(partial_sum, "rep")
    own_rows = lax.dynamic_slice_in_dim(
        summed_rows, lax.axis_index("rep") * slab_rows, slab_rows, 0
    )
    hidden_out = own_rows.astype(jnp.bfloat16)
    gathered = lax.all_gather(cotangent, "rep", axis=0, tiled=True)
    grad_tiles = gathered.reshape(-1, tile_size, gathered.shape[1])
    contrib = jnp.einsum("rmab,raf->rmbf", values, grad_tiles, preferred_element_type=jnp.float32)
    col_tiles = z_tiles.shape[0]
    present = jnp.arange(slot_count)[None, :] < counts[:, None]
    live = jnp.where(present[:, :, None, None], contrib, jnp.zeros((), jnp.float32))
    flat_live = live.reshape(-1, tile_size, live.shape[3])
    flat_columns = columns.reshape(-1)
    spread = (
        jnp.zeros((col_tiles, tile_size, live.shape[3]), jnp.float32)
        .at[flat_columns]
        .add(flat_live)
    )
    spread = spread.reshape(col_tiles * tile_size, spread.shape[2])
    z_grad = lax.psum_scatter(spread, "row", scatter_dimension=0, tiled=True)
    grad_low = z_grad.astype(jnp.bfloat16)
    feature_grad = jnp.dot(grad_low, weight.T, preferred_element_type=jnp.float32).astype(
        jnp.bfloat16
    )
    local_grad = jnp.einsum("nf,ng->fg", reordered, grad_low, preferred_element_type=jnp.float32)
    node_total = slab_rows * lax.axis_size("row") * lax.axis_size("rep")
    weight_grad = lax.psum(local_grad, ("row", "rep")) * (1.0 / math.sqrt(node_total))
    return (hidden_out, feature_grad, weight_grad)


def solution(mesh):
    return jax.shard_map(
        shards,
        mesh=mesh,
        in_specs=(
            P(("row", "rep"), None),
            P(("row", "rep"), None),
            P(),
            P("row", "rep", None, None, None),
            P("row", "rep", None),
            P("row", "rep"),
            P(("row", "rep"), None),
        ),
        out_specs=(P(("row", "rep"), None), P(("row", "rep"), None), P()),
        check_vma=False,
    )
```

profile of v0, /device:TPU:0, one launch (start us, length us, event | category | flops | bytes accessed | tf_op | source)
XLA Modules:
  0.0 278.6 jit_solution(692016063771134414)
XLA Ops:
  7.2 0.7 all-gather.2.cloned.1.call-update
  8.0 0.7 compare_select_fusion.3
  8.6 0.8 copy.14
  9.4 0.7 reduce
  10.2 0.1 reshape.154
  10.3 0.7 compare_and_fusion.1
  11.0 0.1 copy.12
  11.1 0.7 fusion.15
  11.8 1.9 gather_fusion
  13.8 1.0 convolution_convert_fusion.1
  14.8 12.7 %all_gather.6 = bf16[3072,128]{1,0:T(8,128)(2,1)S(1)} all-gather(bf16[768,128]{1,0:T(8,128)(2,1)S(1)} %convolution_convert_fusion.1), channel_id=1, replica_groups=mesh['row'=4,'rep'=8] {'row'}, dimensions={0}, use_global_device_ids=true | all-gather | bytes 983040 | tf_op jit(solution)/shard_map/all_gather | solution.py:28
  27.5 8.1 %gather_fusion.1 = bf16[192,128,128]{2,1,0:T(8,128)(2,1)} fusion(bf16[24,128,128]{2,1,0:T(8,128)(2,1)S(1)} %bitcast.40, s32[1024]{0:T(1024)S(1)} %pad_clamp_fusion), kind=kCustom, calls=%fused_computation.1 | custom fusion | bytes 12583680 | tf_op jit(solution)/shard_map/jit(_take)/gather | solution.py:12
  35.6 8.2 %fusion.2 = f32[48,128,128,1]{1,2,3,0:T(8,128)} fusion(bf16[48,1,4,128,128]{4,3,2,1,0:T(8,128)(2,1)} %param.10, bf16[48,4,128,128]{3,2,1,0:T(8,128)(2,1)} %bitcast.42, pred[48,4]{1,0:T(8,128)(4,1)S(1)} %copy.12, pred[48,4]{1,0:T(8,128)(4,1)S(1)} %iota_compare_fusion), kind=kOutput, calls=%fused_computation.5 | convolution fusion | flops 811597824 | bytes 15729024 | tf_op jit(solution)/shard_map/rmab,rmbf->raf/dot_general | solution.py:15
  43.8 0.1 reshape_squeeze.3
  44.0 10.4 %broadcast_select_fusion = f32[48,4,128,128]{3,2,1,0:T(8,128)} fusion(pred[48,4]{1,0:T(8,128)(4,1)S(1)} %iota_compare_fusion, bf16[48,128,128,1]{2,1,3,0:T(8,128)(2,1)} %bitcast.44, bf16[48,1,4,128,128]{4,3,2,1,0:T(8,128)(2,1)} %param.10), kind=kOutput, calls=%fused_computation.7 | convolution fusion | flops 808452096 | bytes 20447424 | tf_op jit(solution)/shard_map/rmab,raf->rmbf/dot_general | solution.py:38
  54.3 0.2 broadcast_in_dim.56
  54.5 25.3 %scatter_fusion = f32[24,128,128]{2,1,0:T(8,128)S(1)} fusion(f32[24,128,128]{2,1,0:T(8,128)S(1)} %broadcast_in_dim.56, s32[192]{0:T(256)S(1)} %bitcast.45, f32[192,128,128]{2,1,0:T(8,128)} %bitcast.41), kind=kCustom, calls=%fused_computation.2 | custom fusion | flops 3145728 | bytes 37749504 | tf_op jit(solution)/shard_map/scatter-add | solution.py:47
  79.8 1.1 copy-done.1
  81.1 70.2 %all-reduce.4 = bf16[6144,128]{1,0:T(8,128)(2,1)S(1)} all-reduce(f32[6144,128]{1,0:T(8,128)} %bitcast.43), channel_id=1, replica_groups=mesh['row'=4,'rep'=8] {'rep'}, use_global_device_ids=true, to_apply=%region_0.1 | all-reduce | flops 786432 | bytes 4718592 | tf_op jit(solution)/shard_map/psum | solution.py:31
  151.2 0.7 dynamic-slice_convert_fusion
  151.9 2.0 fusion.12
  154.0 1.9 convolution_convert_fusion
  155.9 114.8 %all-reduce.3.cloned.1.call-done = f32[128,128]{1,0:T(8,128)} async-done(((f32[128,128]{1,0:T(8,128)}), f32[128,128]{1,0:T(8,128)}) %all-reduce.3.cloned.1.call-update) | async-done | bytes 65552 | tf_op jit(solution)/shard_map/psum | solution.py:57
  270.6 1.5 broadcast_multiply_fusion
  (20 shorter events, 0.4 us)
Async XLA Ops:
  7.2 4.7 %copy-start = (bf16[768,128]{1,0:T(8,128)(2,1)S(1)}, bf16[768,128]{1,0:T(8,128)(2,1)}, u32[]{:S(2)}) copy-start(bf16[768,128]{1,0:T(8,128)(2,1)} %param.7) | copy-start | bytes 589828
  7.2 36.8 %all-gather.2.cloned.1.call-start = ((), (), s32[]{:S(2)}) async-start(), calls=%async_computation.1 | async-start | bytes 1769472 | tf_op jit(solution)/shard_map/all_gather | solution.py:36
  7.9 144.0 %reduce-scatter.2.cloned.1.call-start = ((), (), s32[]{:S(2)}) async-start(), calls=%async_computation.2 | async-start | bytes 1966080 | tf_op jit(solution)/shard_map/reduce_scatter | solution.py:50
  27.5 8.1 %copy-start.3 = (s32[48,1]{0,1:T(1,128)S(1)}, s32[48,1]{0,1:T(1,128)}, u32[]{:S(2)}) copy-start(s32[48,1]{0,1:T(1,128)} %param.12) | copy-start | bytes 580
  79.8 1.2 copy-start.1
  79.8 74.1 %copy-start.2 = (bf16[128,128]{1,0:T(8,128)(2,1)S(1)}, bf16[128,128]{1,0:T(8,128)(2,1)}, u32[]{:S(2)}) copy-start(bf16[128,128]{1,0:T(8,128)(2,1)} %param.9) | copy-start | bytes 98308
  81.0 189.6 %all-reduce.3.cloned.1.call-start = ((), (), s32[]{:S(2)}) async-start(), calls=%async_computation.3 | async-start | bytes 131072 | tf_op jit(solution)/shard_map/psum | solution.py:57
Sparse Core Ops, SparseCore 0:
  9.7 27.7 all-gather.1
  81.1 31.5 reduce-scatter.1
  154.1 116.5 all-reduce.2
where the time goes:
time: 281 us; the launch traced here: 279 us
  waiting for transfers between devices  116 us (41%)
  blocking collectives  82.8 us (29%)
  other arithmetic  29.7 us (11%)
  matrix products  23.5 us (8%)
  between operations  13.9 us (5%)
  local copies, waits for them, and re-layouts  13.1 us (5%)
    psum x1, waiting for transfers between devices, shards(): lax.psum(local_grad, ('row', 'rep')) * (1.0 / math.sqrt(node_total))  115 us
    psum x1, blocking collectives, shards(): summed_rows = lax.psum(partial_sum, 'rep')  70.2 us
    scatter-add x1, other arithmetic, shards(): spread = jnp.zeros((col_tiles, tile_size, live.shape[3]), jnp.float32).at...  25.3 us
    all_gather x1, blocking collectives, shards(): gathered_z = lax.all_gather(projected, 'row', axis=0, tiled=True)  12.7 us
    dot_general x1, matrix products, shards(): jnp.einsum('rmab,raf->rmbf', values, grad_tiles, preferred_element_type=j...  10.4 us
    dot_general x1, matrix products, aggregate(): jnp.einsum('rmab,rmbf->raf', values, masked, preferred_element_type=jnp.f...  8.19 us
    gather x1, local copies, waits for them, and re-layouts, aggregate(): picked = jnp.take(z_tiles, columns, axis=0)  8.07 us
  transfers between devices with their start and end apart: 3, of which 1 were waited for; matrix products, arithmetic and copies ran while one was open for 9% of the time, Pallas kernels for 0%

commit v1 on v0

v1 whole, which is shorter than its diff:
```python
import functools
import math

import jax
import jax.numpy as jnp
from jax import lax
from jax.experimental import pallas as pl
from jax.experimental.pallas import tpu as pltpu
from jax.sharding import PartitionSpec as P

MESH = pl.DeviceIdType.MESH
VMEM_LIMIT = 52 * 1024 * 1024
F32 = jnp.float32
BF16 = jnp.bfloat16


def remote(src, dst, send, recv, device):
    return pltpu.make_async_remote_copy(
        src_ref=src, dst_ref=dst, send_sem=send, recv_sem=recv, device_id=device, device_id_type=MESH
    )


def enter(devices):
    barrier = pltpu.get_barrier_semaphore()
    for device in devices:
        pl.semaphore_signal(barrier, inc=1, device_id=device, device_id_type=MESH)
    pl.semaphore_wait(barrier, len(devices))


def forward_kernel(
    n_row, n_rep, feat, order, weight, cols, counts, cot, vals_hbm,
    x_all, c_all, pair_out,
    vals, z, to_sib, from_sib,
    vals_sem, x_send, x_recv, c_send, c_recv, f_send, f_recv, h_send, h_recv,
):
    row, rep = lax.axis_index("row"), lax.axis_index("rep")
    places = n_rep // 2
    core, place = lax.rem(rep, 2), rep // 2
    slab = feat.shape[0]
    tile = z.shape[1]
    per_slab = slab // tile
    slots = cols.shape[2]
    sibling = (row, place * 2 + 1 - core)
    row_peers = [(lax.rem(row + d, n_row), rep) for d in range(1, n_row)]
    rep_peers = [(row, lax.rem(place + d, places) * 2 + core) for d in range(1, places)]
    load = pltpu.make_async_copy(vals_hbm, vals, vals_sem)
    load.start()
    enter([sibling] + row_peers + rep_peers)

    started = []
    for d, peer in enumerate(rep_peers, 1):
        copy = remote(cot, c_all.at[rep], c_send.at[d], c_recv.at[d], peer)
        copy.start()
        started.append(copy)
    own_to_sib = remote(cot, c_all.at[rep], f_send.at[0], f_recv.at[0], sibling)
    own_to_sib.start()
    started.append(own_to_sib)
    c_all[rep] = cot[...]

    lane = lax.broadcasted_iota(jnp.int32, (tile, slab), 1)
    for t in range(per_slab):
        piece = order[0:1, t * tile : (t + 1) * tile]
        column = jnp.transpose(jnp.broadcast_to(piece, (tile, tile)))
        wide = jnp.concatenate([column] * per_slab, axis=1)
        pick = jnp.where(wide == lane, 1.0, 0.0).astype(BF16)
        x_all[row, pl.ds(t * tile, tile), :] = jnp.dot(
            pick, feat[...], preferred_element_type=F32
        ).astype(BF16)
    x_copies = []
    for d, peer in enumerate(row_peers, 1):
        copy = remote(x_all.at[row], x_all.at[row], x_send.at[d], x_recv.at[d], peer)
        copy.start()
        x_copies.append(copy)
    started.extend(x_copies)

    def project(owner):
        for t in range(per_slab):
            z[owner * per_slab + t] = jnp.dot(
                x_all[owner, pl.ds(t * tile, tile), :], weight[...], preferred_element_type=F32
            ).astype(BF16)

    z[n_row * per_slab] = jnp.zeros((tile, z.shape[2]), BF16)
    project(row)
    for d in range(1, n_row):
        sender = lax.rem(row - d + n_row, n_row)
        remote(
            x_all.at[sender], x_all.at[sender], x_send.at[d], x_recv.at[d], (sender, rep)
        ).wait_recv()
        project(sender)
    load.wait()

    def block_row(r):
        count = counts[r, 0]
        left = jnp.concatenate([vals[r, m] for m in range(slots)], axis=1)
        picked = [
            z[jnp.where(m < count, cols[r, 0, m], n_row * per_slab)] for m in range(slots)
        ]
        return jnp.dot(left, jnp.concatenate(picked, axis=0), preferred_element_type=F32)

    def for_sibling(q, carry):
        first = (q * 2 + 1 - core) * per_slab
        for t in range(per_slab):
            to_sib[q, pl.ds(t * tile, tile), :] = block_row(first + t).astype(BF16)
        remote(to_sib.at[q], from_sib.at[q], h_send.at[q], h_recv.at[q], sibling).start()
        return carry

    lax.fori_loop(0, places, for_sibling, 0)

    def for_self(q, carry):
        first = (q * 2 + core) * per_slab
        remote(to_sib.at[q], from_sib.at[q], h_send.at[q], h_recv.at[q], sibling).wait()
        for t in range(per_slab):
            rows = pl.ds(t * tile, tile)
            pair_out[q, rows, :] = (block_row(first + t) + from_sib[q, rows, :].astype(F32)).astype(BF16)
        return carry

    lax.fori_loop(0, places, for_self, 0)

    for d in range(1, places):
        sender = lax.rem(place - d + places, places) * 2 + core
        remote(
            c_all.at[sender], c_all.at[sender], c_send.at[d], c_recv.at[d], (row, sender)
        ).wait_recv()
        copy = remote(c_all.at[sender], c_all.at[sender], f_send.at[d], f_recv.at[d], sibling)
        copy.start()
        started.append(copy)
    for d in range(places):
        origin = lax.rem(place - d + places, places) * 2 + 1 - core
        remote(
            c_all.at[origin], c_all.at[origin], f_send.at[d], f_recv.at[d], sibling
        ).wait_recv()
    for copy in started:
        copy.wait_send()


def backward_kernel(cols, counts, vals, cot, x_all, spread, local, total):
    step = pl.program_id(0)
    rows, slots, tile = vals.shape[0], vals.shape[1], vals.shape[2]
    tiles = total.shape[0] - 1

    @pl.when(step == 0)
    def _():
        total[...] = jnp.zeros_like(total)

    for k in range(rows):
        r = step * rows + k
        count = counts[r, 0]
        wide = jnp.concatenate([vals[k, m] for m in range(slots)], axis=1)
        terms = lax.dot_general(
            cot[k], wide, (((0,), (0,)), ((), ())), preferred_element_type=F32
        )
        for m in range(slots):
            at = jnp.where(m < count, cols[r, 0, m], tiles)
            total[at] = total[at] + terms[:, m * tile : (m + 1) * tile]

    @pl.when(step == pl.num_programs(0) - 1)
    def _():
        acc = jnp.zeros(local.shape, F32)
        for c in range(tiles):
            at = pl.ds(c * tile, tile)
            held = total[c]
            spread[at, :] = jnp.transpose(held).astype(BF16)
            acc += jnp.dot(held.astype(BF16), x_all[at, :], preferred_element_type=F32)
        local[...] = jnp.transpose(acc)


def reduce_kernel(
    n_row, n_rep, scale, pair, spread, local, weight,
    hidden, feature_grad, weight_grad,
    h_in, s_in, w_in, w_row,
    h_send, h_recv, s_send, s_recv, a_send, a_recv, b_send, b_recv, g_send, g_recv,
):
    row, rep = lax.axis_index("row"), lax.axis_index("rep")
    places = n_rep // 2
    core, place = lax.rem(rep, 2), rep // 2
    part = local.shape[0] // n_rep
    row_peers = [(lax.rem(row + d, n_row), rep) for d in range(1, n_row)]
    all_peers = [(row, lax.rem(rep + d, n_rep)) for d in range(1, n_rep)]
    enter(row_peers + all_peers)

    def piece(index):
        return pl.ds(pl.multiple_of(index * part, part), part)

    started = []

    def send(src, dst, send_sem, recv_sem, peer):
        copy = remote(src, dst, send_sem, recv_sem, peer)
        copy.start()
        started.append(copy)

    for d, peer in enumerate(all_peers, 1):
        send(local.at[piece(peer[1])], w_in.at[rep], a_send.at[d], a_recv.at[d], peer)
    for d, peer in enumerate(row_peers, 1):
        send(spread.at[peer[0]], s_in.at[row], s_send.at[d], s_recv.at[d], peer)
    for d in range(1, places):
        other = lax.rem(place + d, places)
        send(pair.at[other], h_in.at[place], h_send.at[d], h_recv.at[d], (row, other * 2 + core))

    w_in[rep] = local[piece(rep), :]
    for d in range(1, n_rep):
        sender = lax.rem(rep - d + n_rep, n_rep)
        remote(
            local.at[piece(rep)], w_in.at[sender], a_send.at[d], a_recv.at[d], (row, sender)
        ).wait_recv()
    w_row[row] = jnp.sum(w_in[...], axis=0)
    for d, peer in enumerate(row_peers, 1):
        send(w_row.at[row], w_row.at[row], b_send.at[d], b_recv.at[d], peer)
    for d in range(1, n_row):
        sender = lax.rem(row - d + n_row, n_row)
        remote(
            w_row.at[sender], w_row.at[sender], b_send.at[d], b_recv.at[d], (sender, rep)
        ).wait_recv()
    weight_grad[piece(rep), :] = jnp.sum(w_row[...], axis=0) * scale
    for d, peer in enumerate(all_peers, 1):
        send(
            weight_grad.at[piece(rep)], weight_grad.at[piece(rep)], g_send.at[d], g_recv.at[d], peer
        )

    grad = spread[row].astype(F32)
    for d in range(1, n_row):
        sender = lax.rem(row - d + n_row, n_row)
        remote(
            spread.at[row], s_in.at[sender], s_send.at[d], s_recv.at[d], (sender, rep)
        ).wait_recv()
        grad += s_in[sender].astype(F32)
    feature_grad[...] = lax.dot_general(
        grad.astype(BF16), weight[...], (((1,), (1,)), ((), ())), preferred_element_type=F32
    ).astype(BF16)

    rows = pair[place].astype(F32)
    for d in range(1, places):
        sender = lax.rem(place - d + places, places)
        remote(
            pair.at[place], h_in.at[sender], h_send.at[d], h_recv.at[d], (row, sender * 2 + core)
        ).wait_recv()
        rows += h_in[sender].astype(F32)
    hidden[...] = rows.astype(BF16)
    for d in range(1, n_rep):
        sender = lax.rem(rep - d + n_rep, n_rep)
        remote(
            weight_grad.at[piece(sender)], weight_grad.at[piece(sender)],
            g_send.at[d], g_recv.at[d], (row, sender),
        ).wait_recv()
    for copy in started:
        copy.wait_send()


def solution(mesh):
    n_row, n_rep = mesh.shape["row"], mesh.shape["rep"]
    places = n_rep // 2
    vmem = pl.BlockSpec(memory_space=pltpu.VMEM)
    smem = pl.BlockSpec(memory_space=pltpu.SMEM)
    dma = pltpu.SemaphoreType.DMA

    def shards(features, node_order, weight, tile_vals, tile_cols, row_counts, cotangent):
        slab, width = features.shape
        depth = weight.shape[1]
        tile_rows, _, slots, tile, _ = tile_vals.shape
        tiles = n_row * slab // tile
        vals = tile_vals.reshape(tile_rows, slots, tile, tile)
        shape = jax.ShapeDtypeStruct
        x_all, c_all, pair = pl.pallas_call(
            functools.partial(forward_kernel, n_row, n_rep),
            name="forward",
            out_shape=(
                shape((n_row, slab, width), BF16),
                shape((n_rep, slab, depth), BF16),
                shape((places, slab, depth), BF16),
            ),
            in_specs=[vmem, vmem, vmem, smem, smem, vmem, pl.BlockSpec(memory_space=pl.ANY)],
            out_specs=(vmem, vmem, vmem),
            scratch_shapes=[
                pltpu.VMEM(vals.shape, BF16),
                pltpu.VMEM((tiles + 1, tile, depth), BF16),
                pltpu.VMEM((places, slab, depth), BF16),
                pltpu.VMEM((places, slab, depth), BF16),
                dma,
                dma((n_row,)), dma((n_row,)),
                dma((places,)), dma((places,)),
                dma((places,)), dma((places,)),
                dma((places,)), dma((places,)),
            ],
            compiler_params=pltpu.CompilerParams(
                collective_id=0, has_side_effects=True, vmem_limit_bytes=VMEM_LIMIT
            ),
        )(features, node_order, weight, tile_cols, row_counts, cotangent, vals)

        chunk = 8
        spread, local = pl.pallas_call(
            backward_kernel,
            name="backward",
            grid=(tile_rows // chunk,),
            out_shape=(shape((tiles * tile, depth), BF16), shape((width, depth), F32)),
            in_specs=[
                smem, smem,
                pl.BlockSpec((chunk, slots, tile, tile), lambda i: (i, 0, 0, 0)),
                pl.BlockSpec((chunk, tile, depth), lambda i: (i, 0, 0)),
                pl.BlockSpec((tiles * tile, width), lambda i: (0, 0)),
            ],
            out_specs=(
                pl.BlockSpec((tiles * tile, depth), lambda i: (0, 0)),
                pl.BlockSpec((width, depth), lambda i: (0, 0)),
            ),
            scratch_shapes=[pltpu.VMEM((tiles + 1, depth, tile), F32)],
            compiler_params=pltpu.CompilerParams(vmem_limit_bytes=VMEM_LIMIT),
        )(
            tile_cols, row_counts, vals,
            c_all.reshape(tile_rows, tile, depth), x_all.reshape(tiles * tile, width),
        )

        nodes = slab * n_row * n_rep
        part = width // n_rep
        return pl.pallas_call(
            functools.partial(reduce_kernel, n_row, n_rep, 1.0 / math.sqrt(nodes)),
            name="reduce",
            out_shape=(
                shape((slab, depth), BF16),
                shape((slab, width), BF16),
                shape((width, depth), F32),
            ),
            in_specs=[vmem] * 4,
            out_specs=(vmem,) * 3,
            scratch_shapes=[
                pltpu.VMEM((places, slab, depth), BF16),
                pltpu.VMEM((n_row, slab, depth), BF16),
                pltpu.VMEM((n_rep, part, depth), F32),
                pltpu.VMEM((n_row, part, depth), F32),
                dma((places,)), dma((places,)),
                dma((n_row,)), dma((n_row,)),
                dma((n_rep,)), dma((n_rep,)),
                dma((n_row,)), dma((n_row,)),
                dma((n_rep,)), dma((n_rep,)),
            ],
            compiler_params=pltpu.CompilerParams(
                collective_id=1, has_side_effects=True, vmem_limit_bytes=VMEM_LIMIT
            ),
        )(pair, spread.reshape(n_row, slab, depth), local, weight)

    return jax.shard_map(
        shards,
        mesh=mesh,
        in_specs=(
            P(("row", "rep"), None),
            P(("row", "rep"), None),
            P(),
            P("row", "rep", None, None, None),
            P("row", "rep", None),
            P("row", "rep"),
            P(("row", "rep"), None),
        ),
        out_specs=(P(("row", "rep"), None), P(("row", "rep"), None), P()),
        check_vma=False,
    )
```

time: 281 us -> 67.8 us (0.24)
  waiting for transfers between devices: 116 us -> 0 us
  blocking collectives: 82.8 us -> 0 us
  Pallas kernels: 0 us -> 59.1 us
  other arithmetic: 29.7 us -> 0 us
  matrix products: 23.5 us -> 0 us
  between operations: 13.9 us -> 0.68 us
  local copies, waits for them, and re-layouts: 13.1 us -> 7.67 us
    psum x1 -> x0, waiting for transfers between devices: 115 us -> none  [shards(): lax.psum(local_grad, ('row', 'rep')) * (1.0 / math.sqrt(node_total))]
    psum x1 -> x0, blocking collectives: 70.2 us -> none  [shards(): summed_rows = lax.psum(partial_sum, 'rep')]
    pallas_call x0 -> x3, Pallas kernels: none -> 59.1 us  [the longest x1 27.3 us: shards(): pl.pallas_call(functools.partial(reduce_kernel, n_row, n_rep, 1.0 / math....]
    scatter-add x1 -> x0, other arithmetic: 25.3 us -> none  [shards(): spread = jnp.zeros((col_tiles, tile_size, live.shape[3]), jnp.float32).at...]
    dot_general x5 -> x0, matrix products: 23.5 us -> none  [the longest x1 10.4 us: shards(): jnp.einsum('rmab,raf->rmbf', values, grad_tiles, preferred_element_type=j...]
    all_gather x1 -> x0, blocking collectives: 12.7 us -> none  [shards(): gathered_z = lax.all_gather(projected, 'row', axis=0, tiled=True)]
    gather x2 -> x0, local copies, waits for them, and re-layouts: 9.95 us -> none  [the longest x1 8.07 us: aggregate(): picked = jnp.take(z_tiles, columns, axis=0)]
    unnamed x9 -> x19, local copies, waits for them, and re-layouts: 1.92 us -> 7.67 us
  transfers between devices with their start and end apart: 3 -> 0, of which waited for: 1 -> 0; matrix products, arithmetic and copies ran while one was open for 9% -> 0% of each run, Pallas kernels for 0% -> 0%
where the time goes in v1:
time: 67.8 us; the launch traced here: 67.4 us
  Pallas kernels  59.1 us (87%)
  local copies, waits for them, and re-layouts  7.67 us (11%)
  between operations  0.68 us (1%)
    pallas_call x1, Pallas kernels, shards(): pl.pallas_call(functools.partial(reduce_kernel, n_row, n_rep, 1.0 / math....  27.3 us
    pallas_call x1, Pallas kernels, shards(): pl.pallas_call(functools.partial(forward_kernel, n_row, n_rep), name='for...  25.1 us
    unnamed x19, local copies, waits for them, and re-layouts  7.67 us
    pallas_call x1, Pallas kernels, shards(): pl.pallas_call(backward_kernel, name='backward', grid=(tile_rows // chunk...  6.69 us

profile of v1, /device:TPU:0, one launch (start us, length us, event | category | flops | bytes accessed | tf_op | source)
XLA Modules:
  0.0 67.4 jit_solution(16517021186597087337)
XLA Ops:
  0.6 0.8 %copy.10.cols = s32[48,1,4]{2,1,0:T(1,128)S(1)} copy(s32[48,1,4]{0,2,1:T(4,128)} %param.11) | data formatting | bytes 1536 | tf_op args[4]
  1.4 0.7 %copy.11.counts = s32[48,1]{1,0:T(8,128)S(1)} copy(s32[48,1]{0,1:T(1,128)} %param.12) | data formatting | bytes 384 | tf_op args[5]
  2.1 0.0 copy-start.2
  2.1 0.9 %copy-done.2 = bf16[768,128]{1,0:T(8,128)(2,1)S(1)} copy-done((bf16[768,128]{1,0:T(8,128)(2,1)S(1)}, bf16[768,128]{1,0:T(8,128)(2,1)}, u32[]{:S(2)}) %copy-start.2) | copy-done | bytes 196632
  3.1 0.0 copy-start.3
  3.1 0.9 %copy-done.3 = bf16[768,128]{1,0:T(8,128)(2,1)S(1)} copy-done((bf16[768,128]{1,0:T(8,128)(2,1)S(1)}, bf16[768,128]{1,0:T(8,128)(2,1)}, u32[]{:S(2)}) %copy-start.3) | copy-done | bytes 196632
  4.0 0.0 copy-start.4
  4.0 0.8 %copy-done.4 = bf16[128,128]{1,0:T(8,128)(2,1)S(1)} copy-done((bf16[128,128]{1,0:T(8,128)(2,1)S(1)}, bf16[128,128]{1,0:T(8,128)(2,1)}, u32[]{:S(2)}) %copy-start.4) | copy-done | bytes 32792
  4.8 0.0 copy-start.6
  4.8 0.7 %copy-done.6 = s32[1,768]{1,0:T(1,128)S(1)} copy-done((s32[1,768]{1,0:T(1,128)S(1)}, s32[1,768]{1,0:T(1,128)}, u32[]{:S(2)}) %copy-start.6) | copy-done | bytes 3096
  5.4 0.0 copy-start.5
  5.4 25.1 %forward.1 = (bf16[4,768,128]{2,1,0:T(8,128)(2,1)S(1)}, bf16[8,768,128]{2,1,0:T(8,128)(2,1)}, bf16[4,768,128]{2,1,0:T(8,128)(2,1)}) custom-call(bf16[768,128]{1,0:T(8,128)(2,1)S(1)} %copy-done.2, s32[1,768]{1,0:T(1,128)S(1)} %copy-done.6, bf16[128,128]{1,0:T(8,128)(2,1)S(1)} %copy-done.4, s32[48,1,4]{2,1,0:T(1,128)S(1)} %copy.10.cols, ...), custom_call_target="tpu_custom_call" | custom-call | tf_op jit(solution)/shard_map/forward/pallas_call | solution.py:262
  30.5 0.0 copy-start
  30.5 6.7 %backward.1 = (bf16[3072,128]{1,0:T(8,128)(2,1)S(1)}, f32[128,128]{1,0:T(8,128)S(1)}) custom-call(s32[48,1,4]{2,1,0:T(1,128)S(1)} %copy.10.cols, s32[48,1]{1,0:T(8,128)S(1)} %copy.11.counts, bf16[48,4,128,128]{3,2,1,0:T(8,128)(2,1)} %bitcast.7, bf16[48,128,128]{2,1,0:T(8,128)(2,1)} %bitcast.8, bf16[3072,128]{1,0:T(8,128)(2,1)S(1)} %bitcast.4), custom_call_target="tpu_custom_call" | custom-call | tf_op jit(solution)/shard_map/backward/pallas_call | solution.py:289
  37.2 0.0 copy-start.1
  37.2 0.9 %copy-done.1 = bf16[3072,128]{1,0:T(8,128)(2,1)} copy-done((bf16[3072,128]{1,0:T(8,128)(2,1)}, bf16[3072,128]{1,0:T(8,128)(2,1)S(1)}, u32[]{:S(2)}) %copy-start.1) | copy-done | bytes 786456
  38.1 0.0 copy-done.5
  38.1 0.0 copy-done
  38.1 27.3 %reduce.1 = (bf16[768,128]{1,0:T(8,128)(2,1)S(1)}, bf16[768,128]{1,0:T(8,128)(2,1)S(1)}, f32[128,128]{1,0:T(8,128)S(1)}) custom-call(bf16[4,768,128]{2,1,0:T(8,128)(2,1)S(1)} %copy-done, bf16[4,768,128]{2,1,0:T(8,128)(2,1)} %bitcast.5, f32[128,128]{1,0:T(8,128)S(1)} %get-tuple-element.12.local, bf16[128,128]{1,0:T(8,128)(2,1)S(1)} %copy-done.5), custom_call_target="tpu_custom_call" | custom-call | tf_op jit(solution)/shard_map/reduce/pallas_call | solution.py:313
  65.4 0.7 %copy.17 = bf16[768,128]{1,0:T(8,128)(2,1)} copy(bf16[768,128]{1,0:T(8,128)(2,1)S(1)} %get-tuple-element.16) | data formatting | bytes 393216
  66.1 0.7 %copy.18 = bf16[768,128]{1,0:T(8,128)(2,1)} copy(bf16[768,128]{1,0:T(8,128)(2,1)S(1)} %get-tuple-element.17) | data formatting | bytes 393216
  66.8 0.6 copy.19
Async XLA Ops:
  2.1 0.9 %copy-start.2 = (bf16[768,128]{1,0:T(8,128)(2,1)S(1)}, bf16[768,128]{1,0:T(8,128)(2,1)}, u32[]{:S(2)}) copy-start(bf16[768,128]{1,0:T(8,128)(2,1)} %feat.1) | copy-start | bytes 589828
  3.1 0.9 %copy-start.3 = (bf16[768,128]{1,0:T(8,128)(2,1)S(1)}, bf16[768,128]{1,0:T(8,128)(2,1)}, u32[]{:S(2)}) copy-start(bf16[768,128]{1,0:T(8,128)(2,1)} %cot.1) | copy-start | bytes 589828
  4.0 0.8 %copy-start.4 = (bf16[128,128]{1,0:T(8,128)(2,1)S(1)}, bf16[128,128]{1,0:T(8,128)(2,1)}, u32[]{:S(2)}) copy-start(bf16[128,128]{1,0:T(8,128)(2,1)} %weight.3) | copy-start | bytes 98308
  4.8 0.7 %copy-start.6 = (s32[1,768]{1,0:T(1,128)S(1)}, s32[1,768]{1,0:T(1,128)}, u32[]{:S(2)}) copy-start(s32[1,768]{1,0:T(1,128)} %order.1) | copy-start | bytes 9220
  5.4 32.7 %copy-start.5 = (bf16[128,128]{1,0:T(8,128)(2,1)S(1)}, bf16[128,128]{1,0:T(8,128)(2,1)}, u32[]{:S(2)}) copy-start(bf16[128,128]{1,0:T(8,128)(2,1)} %weight.3) | copy-start | bytes 98308
  30.5 7.6 %copy-start = (bf16[4,768,128]{2,1,0:T(8,128)(2,1)S(1)}, bf16[4,768,128]{2,1,0:T(8,128)(2,1)}, u32[]{:S(2)}) copy-start(bf16[4,768,128]{2,1,0:T(8,128)(2,1)} %get-tuple-element.8.pair) | copy-start | bytes 2359300
  37.2 0.9 %copy-start.1 = (bf16[3072,128]{1,0:T(8,128)(2,1)}, bf16[3072,128]{1,0:T(8,128)(2,1)S(1)}, u32[]{:S(2)}) copy-start(bf16[3072,128]{1,0:T(8,128)(2,1)S(1)} %get-tuple-element.11) | copy-start | bytes 2359300

commit v2 on v1

--- a/solution.py
+++ b/solution.py
@@ -9,9 +9,10 @@
 from jax.sharding import PartitionSpec as P
 
 MESH = pl.DeviceIdType.MESH
-VMEM_LIMIT = 52 * 1024 * 1024
+VMEM_LIMIT = 63 * 1024 * 1024
 F32 = jnp.float32
 BF16 = jnp.bfloat16
+HALVES = 2
 
 
 def remote(src, dst, send, recv, device):
@@ -28,35 +29,82 @@
 
 
 def forward_kernel(
-    n_row, n_rep, feat, order, weight, cols, counts, cot, vals_hbm,
+    n_row, n_rep, feat_hbm, order_hbm, weight_hbm, cols, counts, cot, vals_hbm,
     x_all, c_all, pair_out,
-    vals, z, to_sib, from_sib,
-    vals_sem, x_send, x_recv, c_send, c_recv, f_send, f_recv, h_send, h_recv,
+    vals, feat, order, weight, z, to_sib, from_sib,
+    load_sem, x_send, x_recv, r_send, r_recv, l_send, l_recv, f_send, f_recv, h_send, h_recv, p_sem,
 ):
     row, rep = lax.axis_index("row"), lax.axis_index("rep")
     places = n_rep // 2
     core, place = lax.rem(rep, 2), rep // 2
     slab = feat.shape[0]
+    half = slab // HALVES
     tile = z.shape[1]
     per_slab = slab // tile
-    slots = cols.shape[2]
+    slots = cols.shape[1]
     sibling = (row, place * 2 + 1 - core)
     row_peers = [(lax.rem(row + d, n_row), rep) for d in range(1, n_row)]
-    rep_peers = [(row, lax.rem(place + d, places) * 2 + core) for d in range(1, places)]
-    load = pltpu.make_async_copy(vals_hbm, vals, vals_sem)
-    load.start()
-    enter([sibling] + row_peers + rep_peers)
-
-    started = []
-    for d, peer in enumerate(rep_peers, 1):
-        copy = remote(cot, c_all.at[rep], c_send.at[d], c_recv.at[d], peer)
-        copy.start()
-        started.append(copy)
-    own_to_sib = remote(cot, c_all.at[rep], f_send.at[0], f_recv.at[0], sibling)
-    own_to_sib.start()
-    started.append(own_to_sib)
-    c_all[rep] = cot[...]
-
+    right = (row, lax.rem(place + 1, places) * 2 + core)
+    left = (row, lax.rem(place + places - 1, places) * 2 + core)
+    loads = [
+        pltpu.make_async_copy(src, dst, load_sem.at[i])
+        for i, (src, dst) in enumerate(
+            [(feat_hbm, feat), (order_hbm, order), (weight_hbm, weight), (vals_hbm, vals), (cot, c_all.at[rep])]
+        )
+    ]
+    for load in loads:
+        load.start()
+    enter([sibling, left, right] + row_peers)
+
+    def block(index, h):
+        return c_all.at[index, pl.ds(h * half, half)]
+
+    for h in range(HALVES):
+        own = cot.at[pl.ds(h * half, half)]
+
+        @pl.when(place < places - 1)
+        def _():
+            remote(own, block(rep, h), r_send.at[0, h], r_recv.at[0, h], right).start()
+
+        @pl.when(place > 0)
+        def _():
+            remote(own, block(rep, h), l_send.at[0, h], l_recv.at[0, h], left).start()
+
+    for h in range(HALVES):
+        own = cot.at[pl.ds(h * half, half)]
+        remote(own, block(rep, h), f_send.at[place, h], f_recv.at[place, h], sibling).start()
+
+    def relay(step):
+        for h in range(HALVES):
+
+            @pl.when(place >= step)
+            def _():
+                origin = place - step
+                held = block(origin * 2 + core, h)
+                remote(held, held, r_send.at[step - 1, h], r_recv.at[step - 1, h], left).wait_recv()
+                if step < places - 1:
+
+                    @pl.when(place < places - 1)
+                    def _():
+                        remote(held, held, r_send.at[step, h], r_recv.at[step, h], right).start()
+
+                remote(held, held, f_send.at[origin, h], f_recv.at[origin, h], sibling).start()
+
+            @pl.when(place + step < places)
+            def _():
+                origin = place + step
+                held = block(origin * 2 + core, h)
+                remote(held, held, l_send.at[step - 1, h], l_recv.at[step - 1, h], right).wait_recv()
+                if step < places - 1:
+
+                    @pl.when(place > 0)
+                    def _():
+                        remote(held, held, l_send.at[step, h], l_recv.at[step, h], left).start()
+
+                remote(held, held, f_send.at[origin, h], f_recv.at[origin, h], sibling).start()
+
+    for load in loads[:3]:
+        load.wait()
     lane = lax.broadcasted_iota(jnp.int32, (tile, slab), 1)
     for t in range(per_slab):
         piece = order[0:1, t * tile : (t + 1) * tile]
@@ -71,7 +119,6 @@
         copy = remote(x_all.at[row], x_all.at[row], x_send.at[d], x_recv.at[d], peer)
         copy.start()
         x_copies.append(copy)
-    started.extend(x_copies)
 
     def project(owner):
         for t in range(per_slab):
@@ -87,15 +134,16 @@
             x_all.at[sender], x_all.at[sender], x_send.at[d], x_recv.at[d], (sender, rep)
         ).wait_recv()
         project(sender)
-    load.wait()
+    loads[3].wait()
+    relay(1)
 
     def block_row(r):
-        count = counts[r, 0]
-        left = jnp.concatenate([vals[r, m] for m in range(slots)], axis=1)
+        count = counts[0, r]
+        lhs = jnp.concatenate([vals[r, m] for m in range(slots)], axis=1)
         picked = [
-            z[jnp.where(m < count, cols[r, 0, m], n_row * per_slab)] for m in range(slots)
+            z[jnp.where(m < count, cols[0, m, r], n_row * per_slab)] for m in range(slots)
         ]
-        return jnp.dot(left, jnp.concatenate(picked, axis=0), preferred_element_type=F32)
+        return jnp.dot(lhs, jnp.concatenate(picked, axis=0), preferred_element_type=F32)
 
     def for_sibling(q, carry):
         first = (q * 2 + 1 - core) * per_slab
@@ -105,32 +153,42 @@
         return carry
 
     lax.fori_loop(0, places, for_sibling, 0)
+    if places > 2:
+        relay(2)
 
     def for_self(q, carry):
         first = (q * 2 + core) * per_slab
         remote(to_sib.at[q], from_sib.at[q], h_send.at[q], h_recv.at[q], sibling).wait()
         for t in range(per_slab):
             rows = pl.ds(t * tile, tile)
-            pair_out[q, rows, :] = (block_row(first + t) + from_sib[q, rows, :].astype(F32)).astype(BF16)
+            from_sib[q, rows, :] = (block_row(first + t) + from_sib[q, rows, :].astype(F32)).astype(BF16)
+        pltpu.make_async_copy(from_sib.at[q], pair_out.at[q], p_sem.at[q]).start()
         return carry
 
     lax.fori_loop(0, places, for_self, 0)
 
-    for d in range(1, places):
-        sender = lax.rem(place - d + places, places) * 2 + core
-        remote(
-            c_all.at[sender], c_all.at[sender], c_send.at[d], c_recv.at[d], (row, sender)
-        ).wait_recv()
-        copy = remote(c_all.at[sender], c_all.at[sender], f_send.at[d], f_recv.at[d], sibling)
-        copy.start()
-        started.append(copy)
-    for d in range(places):
-        origin = lax.rem(place - d + places, places) * 2 + 1 - core
-        remote(
-            c_all.at[origin], c_all.at[origin], f_send.at[d], f_recv.at[d], sibling
-        ).wait_recv()
-    for copy in started:
+    for step in range(3, places):
+        relay(step)
+
+    for q in range(places):
+        pltpu.make_async_copy(from_sib.at[q], pair_out.at[q], p_sem.at[q]).wait()
+        for h in range(HALVES):
+            held = block(q * 2 + 1 - core, h)
+            remote(held, held, f_send.at[q, h], f_recv.at[q, h], sibling).wait()
+    loads[4].wait()
+    for copy in x_copies:
         copy.wait_send()
+    for step in range(places - 1):
+        for h in range(HALVES):
+            held = block(rep, h)
+
+            @pl.when((place < places - 1) & (place >= step))
+            def _():
+                remote(held, held, r_send.at[step, h], r_recv.at[step, h], right).wait_send()
+
+            @pl.when((place > 0) & (place + step < places))
+            def _():
+                remote(held, held, l_send.at[step, h], l_recv.at[step, h], left).wait_send()
 
 
 def backward_kernel(cols, counts, vals, cot, x_all, spread, local, total):
@@ -144,13 +202,13 @@
 
     for k in range(rows):
         r = step * rows + k
-        count = counts[r, 0]
+        count = counts[0, r]
         wide = jnp.concatenate([vals[k, m] for m in range(slots)], axis=1)
         terms = lax.dot_general(
             cot[k], wide, (((0,), (0,)), ((), ())), preferred_element_type=F32
         )
         for m in range(slots):
-            at = jnp.where(m < count, cols[r, 0, m], tiles)
+            at = jnp.where(m < count, cols[0, m, r], tiles)
             total[at] = total[at] + terms[:, m * tile : (m + 1) * tile]
 
     @pl.when(step == pl.num_programs(0) - 1)
@@ -165,10 +223,10 @@
 
 
 def reduce_kernel(
-    n_row, n_rep, scale, pair, spread, local, weight,
+    n_row, n_rep, scale, pair_hbm, spread, local, weight,
     hidden, feature_grad, weight_grad,
-    h_in, s_in, w_in, w_row,
-    h_send, h_recv, s_send, s_recv, a_send, a_recv, b_send, b_recv, g_send, g_recv,
+    pair, r_in, l_in, r_sum, l_sum, s_in, w_in, w_row,
+    r_send, r_recv, l_send, l_recv, own_sem, s_send, s_recv, a_send, a_recv, b_send, b_recv, g_send, g_recv,
 ):
     row, rep = lax.axis_index("row"), lax.axis_index("rep")
     places = n_rep // 2
@@ -176,6 +234,13 @@
     part = local.shape[0] // n_rep
     row_peers = [(lax.rem(row + d, n_row), rep) for d in range(1, n_row)]
     all_peers = [(row, lax.rem(rep + d, n_rep)) for d in range(1, n_rep)]
+    right = (row, lax.rem(place + 1, places) * 2 + core)
+    left = (row, lax.rem(place + places - 1, places) * 2 + core)
+    half = pair.shape[1] // HALVES
+    own = pltpu.make_async_copy(spread.at[row], s_in.at[row], own_sem.at[0])
+    own.start()
+    load = pltpu.make_async_copy(pair_hbm, pair, own_sem.at[1])
+    load.start()
     enter(row_peers + all_peers)
 
     def piece(index):
@@ -192,10 +257,47 @@
         send(local.at[piece(peer[1])], w_in.at[rep], a_send.at[d], a_recv.at[d], peer)
     for d, peer in enumerate(row_peers, 1):
         send(spread.at[peer[0]], s_in.at[row], s_send.at[d], s_recv.at[d], peer)
-    for d in range(1, places):
-        other = lax.rem(place + d, places)
-        send(pair.at[other], h_in.at[place], h_send.at[d], h_recv.at[d], (row, other * 2 + core))
-
+    def add(held, arrived, q, rows):
+        held[q, rows, :] = (arrived[q, rows, :].astype(F32) + pair[q, rows, :].astype(F32)).astype(BF16)
+
+    def relay(step):
+        to_right = places - 1 + place - step
+        to_left = step - (places - 1) + place
+        for h in range(HALVES):
+            rows = pl.ds(h * half, half)
+
+            @pl.when((to_right > place) & (to_right < places))
+            def _():
+                q = to_right
+                target, sems = r_in.at[q, rows], (r_send.at[q, h], r_recv.at[q, h])
+
+                @pl.when(place == 0)
+                def _():
+                    remote(pair.at[q, rows], target, *sems, right).start()
+
+                @pl.when(place > 0)
+                def _():
+                    remote(target, target, *sems, left).wait_recv()
+                    add(r_sum, r_in, q, rows)
+                    remote(r_sum.at[q, rows], target, *sems, right).start()
+
+            @pl.when((to_left >= 0) & (to_left < place))
+            def _():
+                q = to_left
+                target, sems = l_in.at[q, rows], (l_send.at[q, h], l_recv.at[q, h])
+
+                @pl.when(place == places - 1)
+                def _():
+                    remote(pair.at[q, rows], target, *sems, left).start()
+
+                @pl.when(place < places - 1)
+                def _():
+                    remote(target, target, *sems, right).wait_recv()
+                    add(l_sum, l_in, q, rows)
+                    remote(l_sum.at[q, rows], target, *sems, left).start()
+
+    load.wait()
+    relay(0)
     w_in[rep] = local[piece(rep), :]
     for d in range(1, n_rep):
         sender = lax.rem(rep - d + n_rep, n_rep)
@@ -210,13 +312,16 @@
         remote(
             w_row.at[sender], w_row.at[sender], b_send.at[d], b_recv.at[d], (sender, rep)
         ).wait_recv()
+    if places > 2:
+        relay(1)
     weight_grad[piece(rep), :] = jnp.sum(w_row[...], axis=0) * scale
     for d, peer in enumerate(all_peers, 1):
         send(
             weight_grad.at[piece(rep)], weight_grad.at[piece(rep)], g_send.at[d], g_recv.at[d], peer
         )
 
-    grad = spread[row].astype(F32)
+    own.wait()
+    grad = s_in[row].astype(F32)
     for d in range(1, n_row):
         sender = lax.rem(row - d + n_row, n_row)
         remote(
@@ -227,14 +332,49 @@
         grad.astype(BF16), weight[...], (((1,), (1,)), ((), ())), preferred_element_type=F32
     ).astype(BF16)
 
-    rows = pair[place].astype(F32)
-    for d in range(1, places):
-        sender = lax.rem(place - d + places, places)
-        remote(
-            pair.at[place], h_in.at[sender], h_send.at[d], h_recv.at[d], (row, sender * 2 + core)
-        ).wait_recv()
-        rows += h_in[sender].astype(F32)
-    hidden[...] = rows.astype(BF16)
+    for step in range(2, places - 1):
+        relay(step)
+    for h in range(HALVES):
+        rows = pl.ds(h * half, half)
+
+        @pl.when(place > 0)
+        def _():
+            target = r_in.at[place, rows]
+            remote(target, target, r_send.at[place, h], r_recv.at[place, h], left).wait_recv()
+
+        @pl.when(place < places - 1)
+        def _():
+            target = l_in.at[place, rows]
+            remote(target, target, l_send.at[place, h], l_recv.at[place, h], right).wait_recv()
+
+        @pl.when(place == 0)
+        def _():
+            hidden[rows, :] = (pair[place, rows, :].astype(F32) + l_in[place, rows, :].astype(F32)).astype(BF16)
+
+        @pl.when(place == places - 1)
+        def _():
+            hidden[rows, :] = (pair[place, rows, :].astype(F32) + r_in[place, rows, :].astype(F32)).astype(BF16)
+
+        @pl.when((place > 0) & (place < places - 1))
+        def _():
+            hidden[rows, :] = (
+                pair[place, rows, :].astype(F32)
+                + r_in[place, rows, :].astype(F32)
+                + l_in[place, rows, :].astype(F32)
+            ).astype(BF16)
+
+    for q in range(places):
+        for h in range(HALVES):
+            held = r_sum.at[q, pl.ds(h * half, half)]
+
+            @pl.when(place < q)
+            def _():
+                remote(held, held, r_send.at[q, h], r_recv.at[q, h], right).wait_send()
+
+            @pl.when(place > q)
+            def _():
+                remote(held, held, l_send.at[q, h], l_recv.at[q, h], left).wait_send()
+
     for d in range(1, n_rep):
         sender = lax.rem(rep - d + n_rep, n_rep)
         remote(
@@ -250,6 +390,7 @@
     places = n_rep // 2
     vmem = pl.BlockSpec(memory_space=pltpu.VMEM)
     smem = pl.BlockSpec(memory_space=pltpu.SMEM)
+    hbm = pl.BlockSpec(memory_space=pltpu.HBM)
     dma = pltpu.SemaphoreType.DMA
 
     def shards(features, node_order, weight, tile_vals, tile_cols, row_counts, cotangent):
@@ -258,6 +399,8 @@
         tile_rows, _, slots, tile, _ = tile_vals.shape
         tiles = n_row * slab // tile
         vals = tile_vals.reshape(tile_rows, slots, tile, tile)
+        cols = jnp.transpose(tile_cols, (1, 2, 0))
+        counts = jnp.transpose(row_counts, (1, 0))
         shape = jax.ShapeDtypeStruct
         x_all, c_all, pair = pl.pallas_call(
             functools.partial(forward_kernel, n_row, n_rep),
@@ -267,23 +410,28 @@
                 shape((n_rep, slab, depth), BF16),
                 shape((places, slab, depth), BF16),
             ),
-            in_specs=[vmem, vmem, vmem, smem, smem, vmem, pl.BlockSpec(memory_space=pl.ANY)],
-            out_specs=(vmem, vmem, vmem),
+            in_specs=[hbm, hbm, hbm, smem, smem, hbm, hbm],
+            out_specs=(vmem, hbm, hbm),
             scratch_shapes=[
                 pltpu.VMEM(vals.shape, BF16),
+                pltpu.VMEM(features.shape, BF16),
+                pltpu.VMEM(node_order.shape, jnp.int32),
+                pltpu.VMEM(weight.shape, BF16),
                 pltpu.VMEM((tiles + 1, tile, depth), BF16),
                 pltpu.VMEM((places, slab, depth), BF16),
                 pltpu.VMEM((places, slab, depth), BF16),
-                dma,
+                dma((5,)),
                 dma((n_row,)), dma((n_row,)),
+                dma((places, HALVES)), dma((places, HALVES)),
+                dma((places, HALVES)), dma((places, HALVES)),
+                dma((places, HALVES)), dma((places, HALVES)),
                 dma((places,)), dma((places,)),
-                dma((places,)), dma((places,)),
-                dma((places,)), dma((places,)),
+                dma((places,)),
             ],
             compiler_params=pltpu.CompilerParams(
                 collective_id=0, has_side_effects=True, vmem_limit_bytes=VMEM_LIMIT
             ),
-        )(features, node_order, weight, tile_cols, row_counts, cotangent, vals)
+        )(features, node_order, weight, cols, counts, cotangent, vals)
 
         chunk = 8
         spread, local = pl.pallas_call(
@@ -304,7 +452,7 @@
             scratch_shapes=[pltpu.VMEM((tiles + 1, depth, tile), F32)],
             compiler_params=pltpu.CompilerParams(vmem_limit_bytes=VMEM_LIMIT),
         )(
-            tile_cols, row_counts, vals,
+            cols, counts, vals,
             c_all.reshape(tile_rows, tile, depth), x_all.reshape(tiles * tile, width),
         )
 
@@ -318,14 +466,20 @@
                 shape((slab, width), BF16),
                 shape((width, depth), F32),
             ),
-            in_specs=[vmem] * 4,
+            in_specs=[hbm, hbm, vmem, vmem],
             out_specs=(vmem,) * 3,
             scratch_shapes=[
+                pltpu.VMEM((places, slab, depth), BF16),
+                pltpu.VMEM((places, slab, depth), BF16),
+                pltpu.VMEM((places, slab, depth), BF16),
+                pltpu.VMEM((places, slab, depth), BF16),
                 pltpu.VMEM((places, slab, depth), BF16),
                 pltpu.VMEM((n_row, slab, depth), BF16),
                 pltpu.VMEM((n_rep, part, depth), F32),
                 pltpu.VMEM((n_row, part, depth), F32),
-                dma((places,)), dma((places,)),
+                dma((places, HALVES)), dma((places, HALVES)),
+                dma((places, HALVES)), dma((places, HALVES)),
+                dma((2,)),
                 dma((n_row,)), dma((n_row,)),
                 dma((n_rep,)), dma((n_rep,)),
                 dma((n_row,)), dma((n_row,)),

time: 67.8 us -> 69.3 us (1.022)
  Pallas kernels: 59.1 us -> 63.6 us
  local copies, waits for them, and re-layouts: 7.67 us -> 4.7 us
    pallas_call x1, Pallas kernels: 25.1 us -> 28.4 us  [shards(): pl.pallas_call(functools.partial(forward_kernel, n_row, n_rep), name='for...]
    unnamed x19 -> x3, local copies, waits for them, and re-layouts: 7.67 us -> 4.7 us
    pallas_call x1, Pallas kernels: 6.69 us -> 7.77 us  [shards(): pl.pallas_call(backward_kernel, name='backward', grid=(tile_rows // chunk...]
where the time goes in v2:
time: 69.3 us; the launch traced here: 69 us
  Pallas kernels  63.6 us (92%)
  local copies, waits for them, and re-layouts  4.7 us (7%)
    pallas_call x1, Pallas kernels, shards(): pl.pallas_call(functools.partial(forward_kernel, n_row, n_rep), name='for...  28.4 us
    pallas_call x1, Pallas kernels, shards(): pl.pallas_call(functools.partial(reduce_kernel, n_row, n_rep, 1.0 / math....  27.4 us
    pallas_call x1, Pallas kernels, shards(): pl.pallas_call(backward_kernel, name='backward', grid=(tile_rows // chunk...  7.77 us
    unnamed x3, local copies, waits for them, and re-layouts  4.7 us

profile of v2, /device:TPU:0, one launch (start us, length us, event | category | flops | bytes accessed | tf_op | source)
XLA Modules:
  0.0 69.0 jit_solution(6496980601749275574)
XLA Ops:
  0.6 28.4 %forward.1 = (bf16[4,768,128]{2,1,0:T(8,128)(2,1)}, bf16[8,768,128]{2,1,0:T(8,128)(2,1)}, bf16[4,768,128]{2,1,0:T(8,128)(2,1)}) custom-call(bf16[768,128]{1,0:T(8,128)(2,1)} %feat_hbm.1, s32[1,768]{1,0:T(1,128)} %order_hbm.1, bf16[128,128]{1,0:T(8,128)(2,1)} %weight.1, s32[1,4,48]{2,1,0:T(4,128)} %bitcast.11, s32[1,48]{1,0:T(1,128)} %bitcast.13, ...), custom_call_target="tpu_custom_call" | custom-call | tf_op jit(solution)/shard_map/forward/pallas_call | solution.py:405
  29.1 7.8 %backward.1 = (bf16[3072,128]{1,0:T(8,128)(2,1)}, f32[128,128]{1,0:T(8,128)}) custom-call(s32[1,4,48]{2,1,0:T(4,128)} %bitcast.12, s32[1,48]{1,0:T(1,128)} %bitcast.14, bf16[48,4,128,128]{3,2,1,0:T(8,128)(2,1)} %bitcast.7, bf16[48,128,128]{2,1,0:T(8,128)(2,1)} %bitcast.8, bf16[3072,128]{1,0:T(8,128)(2,1)} %bitcast.9), custom_call_target="tpu_custom_call" | custom-call | tf_op jit(solution)/shard_map/backward/pallas_call | solution.py:437
  36.9 27.4 %reduce.1 = (bf16[768,128]{1,0:T(8,128)(2,1)}, bf16[768,128]{1,0:T(8,128)(2,1)}, f32[128,128]{1,0:T(8,128)}) custom-call(bf16[4,768,128]{2,1,0:T(8,128)(2,1)} %get-tuple-element.8.pair_hbm, bf16[4,768,128]{2,1,0:T(8,128)(2,1)} %bitcast.10, f32[128,128]{1,0:T(8,128)} %get-tuple-element.12.local, bf16[128,128]{1,0:T(8,128)(2,1)} %weight.1), custom_call_target="tpu_custom_call" | custom-call | tf_op jit(solution)/shard_map/reduce/pallas_call | solution.py:461
  64.3 1.6 %copy.13 = bf16[768,128]{1,0:T(8,128)(2,1)} copy(bf16[768,128]{1,0:T(8,128)(2,1)} %get-tuple-element.16) | data formatting | bytes 393216
  65.9 1.6 %copy.14 = bf16[768,128]{1,0:T(8,128)(2,1)} copy(bf16[768,128]{1,0:T(8,128)(2,1)} %get-tuple-element.17) | data formatting | bytes 393216
  67.5 1.5 %copy.15 = f32[128,128]{1,0:T(8,128)} copy(f32[128,128]{1,0:T(8,128)} %get-tuple-element.18) | data formatting | bytes 131072

commit v3 on v2

--- a/solution.py
+++ b/solution.py
@@ -12,6 +12,8 @@
 VMEM_LIMIT = 63 * 1024 * 1024
 F32 = jnp.float32
 BF16 = jnp.bfloat16
+MIDDLE_LIMIT = 63 * 1024 * 1024
+LATER_LIMIT = 40 * 1024 * 1024
 HALVES = 2
 
 
@@ -128,6 +130,7 @@
 
     z[n_row * per_slab] = jnp.zeros((tile, z.shape[2]), BF16)
     project(row)
+    relay(1)
     for d in range(1, n_row):
         sender = lax.rem(row - d + n_row, n_row)
         remote(
@@ -135,7 +138,8 @@
         ).wait_recv()
         project(sender)
     loads[3].wait()
-    relay(1)
+    if places > 2:
+        relay(2)
 
     def block_row(r):
         count = counts[0, r]
@@ -153,8 +157,8 @@
         return carry
 
     lax.fori_loop(0, places, for_sibling, 0)
-    if places > 2:
-        relay(2)
+    if places > 3:
+        relay(3)
 
     def for_self(q, carry):
         first = (q * 2 + core) * per_slab
@@ -167,7 +171,7 @@
 
     lax.fori_loop(0, places, for_self, 0)
 
-    for step in range(3, places):
+    for step in range(4, places):
         relay(step)
 
     for q in range(places):
@@ -255,8 +259,12 @@
 
     for d, peer in enumerate(all_peers, 1):
         send(local.at[piece(peer[1])], w_in.at[rep], a_send.at[d], a_recv.at[d], peer)
-    for d, peer in enumerate(row_peers, 1):
-        send(spread.at[peer[0]], s_in.at[row], s_send.at[d], s_recv.at[d], peer)
+    def send_spread(h):
+        rows = pl.ds(h * half, half)
+        for d, peer in enumerate(row_peers, 1):
+            send(spread.at[peer[0], rows], s_in.at[row, rows], s_send.at[d, h], s_recv.at[d, h], peer)
+
+    send_spread(0)
     def add(held, arrived, q, rows):
         held[q, rows, :] = (arrived[q, rows, :].astype(F32) + pair[q, rows, :].astype(F32)).astype(BF16)
 
@@ -307,33 +315,37 @@
     w_row[row] = jnp.sum(w_in[...], axis=0)
     for d, peer in enumerate(row_peers, 1):
         send(w_row.at[row], w_row.at[row], b_send.at[d], b_recv.at[d], peer)
+    for h in range(1, HALVES):
+        send_spread(h)
+    if places > 2:
+        relay(1)
     for d in range(1, n_row):
         sender = lax.rem(row - d + n_row, n_row)
         remote(
             w_row.at[sender], w_row.at[sender], b_send.at[d], b_recv.at[d], (sender, rep)
         ).wait_recv()
-    if places > 2:
-        relay(1)
     weight_grad[piece(rep), :] = jnp.sum(w_row[...], axis=0) * scale
     for d, peer in enumerate(all_peers, 1):
         send(
             weight_grad.at[piece(rep)], weight_grad.at[piece(rep)], g_send.at[d], g_recv.at[d], peer
         )
 
+    for step in range(2, places - 1):
+        relay(step)
     own.wait()
     grad = s_in[row].astype(F32)
     for d in range(1, n_row):
         sender = lax.rem(row - d + n_row, n_row)
-        remote(
-            spread.at[row], s_in.at[sender], s_send.at[d], s_recv.at[d], (sender, rep)
-        ).wait_recv()
+        for h in range(HALVES):
+            rows = pl.ds(h * half, half)
+            remote(
+                spread.at[row, rows], s_in.at[sender, rows], s_send.at[d, h], s_recv.at[d, h], (sender, rep)
+            ).wait_recv()
         grad += s_in[sender].astype(F32)
     feature_grad[...] = lax.dot_general(
         grad.astype(BF16), weight[...], (((1,), (1,)), ((), ())), preferred_element_type=F32
     ).astype(BF16)
 
-    for step in range(2, places - 1):
-        relay(step)
     for h in range(HALVES):
         rows = pl.ds(h * half, half)
 
@@ -450,7 +462,7 @@
                 pl.BlockSpec((width, depth), lambda i: (0, 0)),
             ),
             scratch_shapes=[pltpu.VMEM((tiles + 1, depth, tile), F32)],
-            compiler_params=pltpu.CompilerParams(vmem_limit_bytes=VMEM_LIMIT),
+            compiler_params=pltpu.CompilerParams(vmem_limit_bytes=MIDDLE_LIMIT),
         )(
             cols, counts, vals,
             c_all.reshape(tile_rows, tile, depth), x_all.reshape(tiles * tile, width),
@@ -480,13 +492,13 @@
                 dma((places, HALVES)), dma((places, HALVES)),
                 dma((places, HALVES)), dma((places, HALVES)),
                 dma((2,)),
-                dma((n_row,)), dma((n_row,)),
+                dma((n_row, HALVES)), dma((n_row, HALVES)),
                 dma((n_rep,)), dma((n_rep,)),
                 dma((n_row,)), dma((n_row,)),
                 dma((n_rep,)), dma((n_rep,)),
             ],
             compiler_params=pltpu.CompilerParams(
-                collective_id=1, has_side_effects=True, vmem_limit_bytes=VMEM_LIMIT
+                collective_id=1, has_side_effects=True, vmem_limit_bytes=LATER_LIMIT
             ),
         )(pair, spread.reshape(n_row, slab, depth), local, weight)
 

time: 69.3 us -> 57.3 us (0.83)
  Pallas kernels: 63.6 us -> 52.3 us
  local copies, waits for them, and re-layouts: 4.7 us -> 3.96 us
    pallas_call x1, Pallas kernels: 27.4 us -> 19.5 us  [shards(): pl.pallas_call(functools.partial(reduce_kernel, n_row, n_rep, 1.0 / math....]
    pallas_call x1, Pallas kernels: 28.4 us -> 25 us  [shards(): pl.pallas_call(functools.partial(forward_kernel, n_row, n_rep), name='for...]
    unnamed x3 -> x11, local copies, waits for them, and re-layouts: 4.7 us -> 3.96 us
where the time goes in v3:
time: 57.3 us; the launch traced here: 57 us
  Pallas kernels  52.3 us (91%)
  local copies, waits for them, and re-layouts  3.96 us (7%)
  between operations  0.68 us (1%)
    pallas_call x1, Pallas kernels, shards(): pl.pallas_call(functools.partial(forward_kernel, n_row, n_rep), name='for...  25 us
    pallas_call x1, Pallas kernels, shards(): pl.pallas_call(functools.partial(reduce_kernel, n_row, n_rep, 1.0 / math....  19.5 us
    pallas_call x1, Pallas kernels, shards(): pl.pallas_call(backward_kernel, name='backward', grid=(tile_rows // chunk...  7.84 us
    unnamed x11, local copies, waits for them, and re-layouts  3.96 us

profile of v3, /device:TPU:0, one launch (start us, length us, event | category | flops | bytes accessed | tf_op | source)
XLA Modules:
  0.0 57.0 jit_solution(2551212846657864455)
XLA Ops:
  0.6 0.0 copy-start.2
  0.6 25.0 %forward.1 = (bf16[4,768,128]{2,1,0:T(8,128)(2,1)}, bf16[8,768,128]{2,1,0:T(8,128)(2,1)}, bf16[4,768,128]{2,1,0:T(8,128)(2,1)}) custom-call(bf16[768,128]{1,0:T(8,128)(2,1)} %feat_hbm.1, s32[1,768]{1,0:T(1,128)} %order_hbm.1, bf16[128,128]{1,0:T(8,128)(2,1)} %weight.1, s32[1,4,48]{2,1,0:T(4,128)} %bitcast.11, s32[1,48]{1,0:T(1,128)} %bitcast.13, ...), custom_call_target="tpu_custom_call" | custom-call | tf_op jit(solution)/shard_map/forward/pallas_call | solution.py:417
  25.7 0.0 copy-start
  25.7 7.8 %backward.1 = (bf16[3072,128]{1,0:T(8,128)(2,1)}, f32[128,128]{1,0:T(8,128)}) custom-call(s32[1,4,48]{2,1,0:T(4,128)} %bitcast.12, s32[1,48]{1,0:T(1,128)} %bitcast.14, bf16[48,4,128,128]{3,2,1,0:T(8,128)(2,1)} %bitcast.8, bf16[48,128,128]{2,1,0:T(8,128)(2,1)} %bitcast.9, bf16[3072,128]{1,0:T(8,128)(2,1)} %bitcast.10), custom_call_target="tpu_custom_call" | custom-call | tf_op jit(solution)/shard_map/backward/pallas_call | solution.py:449
  33.5 0.0 copy-done.2
  33.5 0.0 copy-done
  33.5 0.0 copy-start.1
  33.5 1.1 %copy-done.1 = bf16[3072,128]{1,0:T(8,128)(2,1)S(1)} copy-done((bf16[3072,128]{1,0:T(8,128)(2,1)S(1)}, bf16[3072,128]{1,0:T(8,128)(2,1)}, u32[]{:S(2)}) %copy-start.1) | copy-done | bytes 786456
  34.7 0.0 copy-start.3
  34.7 0.8 %copy-done.3 = f32[128,128]{1,0:T(8,128)S(1)} copy-done((f32[128,128]{1,0:T(8,128)S(1)}, f32[128,128]{1,0:T(8,128)}, u32[]{:S(2)}) %copy-start.3) | copy-done | bytes 65560
  35.5 19.5 %reduce.1 = (bf16[768,128]{1,0:T(8,128)(2,1)S(1)}, bf16[768,128]{1,0:T(8,128)(2,1)S(1)}, f32[128,128]{1,0:T(8,128)S(1)}) custom-call(bf16[4,768,128]{2,1,0:T(8,128)(2,1)S(1)} %copy-done, bf16[4,768,128]{2,1,0:T(8,128)(2,1)S(1)} %bitcast.6, f32[128,128]{1,0:T(8,128)S(1)} %copy-done.3, bf16[128,128]{1,0:T(8,128)(2,1)S(1)} %copy-done.2), custom_call_target="tpu_custom_call" | custom-call | tf_op jit(solution)/shard_map/reduce/pallas_call | solution.py:473
  55.0 0.7 %copy.13 = bf16[768,128]{1,0:T(8,128)(2,1)} copy(bf16[768,128]{1,0:T(8,128)(2,1)S(1)} %get-tuple-element.16) | data formatting | bytes 393216
  55.7 0.7 %copy.14 = bf16[768,128]{1,0:T(8,128)(2,1)} copy(bf16[768,128]{1,0:T(8,128)(2,1)S(1)} %get-tuple-element.17) | data formatting | bytes 393216
  56.4 0.6 %copy.15 = f32[128,128]{1,0:T(8,128)} copy(f32[128,128]{1,0:T(8,128)S(1)} %get-tuple-element.18) | data formatting | bytes 131072
Async XLA Ops:
  0.6 32.9 %copy-start.2 = (bf16[128,128]{1,0:T(8,128)(2,1)S(1)}, bf16[128,128]{1,0:T(8,128)(2,1)}, u32[]{:S(2)}) copy-start(bf16[128,128]{1,0:T(8,128)(2,1)} %weight.1) | copy-start | bytes 98308
  25.7 7.9 %copy-start = (bf16[4,768,128]{2,1,0:T(8,128)(2,1)S(1)}, bf16[4,768,128]{2,1,0:T(8,128)(2,1)}, u32[]{:S(2)}) copy-start(bf16[4,768,128]{2,1,0:T(8,128)(2,1)} %get-tuple-element.8.pair_hbm) | copy-start | bytes 2359300
  33.5 1.1 %copy-start.1 = (bf16[3072,128]{1,0:T(8,128)(2,1)S(1)}, bf16[3072,128]{1,0:T(8,128)(2,1)}, u32[]{:S(2)}) copy-start(bf16[3072,128]{1,0:T(8,128)(2,1)} %get-tuple-element.11) | copy-start | bytes 2359300
  34.7 0.8 %copy-start.3 = (f32[128,128]{1,0:T(8,128)S(1)}, f32[128,128]{1,0:T(8,128)}, u32[]{:S(2)}) copy-start(f32[128,128]{1,0:T(8,128)} %get-tuple-element.12.local) | copy-start | bytes 196612

commit v4 on v3

--- a/solution.py
+++ b/solution.py
@@ -12,7 +12,7 @@
 VMEM_LIMIT = 63 * 1024 * 1024
 F32 = jnp.float32
 BF16 = jnp.bfloat16
-MIDDLE_LIMIT = 63 * 1024 * 1024
+MIDDLE_LIMIT = 52 * 1024 * 1024
 LATER_LIMIT = 40 * 1024 * 1024
 HALVES = 2
 
@@ -33,8 +33,8 @@
 def forward_kernel(
     n_row, n_rep, feat_hbm, order_hbm, weight_hbm, cols, counts, cot, vals_hbm,
     x_all, c_all, pair_out,
-    vals, feat, order, weight, z, to_sib, from_sib,
-    load_sem, x_send, x_recv, r_send, r_recv, l_send, l_recv, f_send, f_recv, h_send, h_recv, p_sem,
+    vals, feat, order, weight, z, to_sib, from_sib, hop_in,
+    load_sem, x_send, x_recv, r_send, r_recv, l_send, l_recv, f_send, f_recv, h_send, h_recv, p_sem, e_send, e_recv,
 ):
     row, rep = lax.axis_index("row"), lax.axis_index("rep")
     places = n_rep // 2
@@ -137,9 +137,9 @@
             x_all.at[sender], x_all.at[sender], x_send.at[d], x_recv.at[d], (sender, rep)
         ).wait_recv()
         project(sender)
+        if d == 1:
+            relay(2)
     loads[3].wait()
-    if places > 2:
-        relay(2)
 
     def block_row(r):
         count = counts[0, r]
@@ -149,30 +149,84 @@
         ]
         return jnp.dot(lhs, jnp.concatenate(picked, axis=0), preferred_element_type=F32)
 
-    def for_sibling(q, carry):
+    def turn(k):
+        return lax.rem(k + places - 1 - place, places)
+
+    def for_sibling(k):
+        q = turn(k)
         first = (q * 2 + 1 - core) * per_slab
         for t in range(per_slab):
             to_sib[q, pl.ds(t * tile, tile), :] = block_row(first + t).astype(BF16)
         remote(to_sib.at[q], from_sib.at[q], h_send.at[q], h_recv.at[q], sibling).start()
-        return carry
-
-    lax.fori_loop(0, places, for_sibling, 0)
-    if places > 3:
-        relay(3)
-
-    def for_self(q, carry):
+
+    def for_self(k):
+        q = turn(k)
         first = (q * 2 + core) * per_slab
         remote(to_sib.at[q], from_sib.at[q], h_send.at[q], h_recv.at[q], sibling).wait()
         for t in range(per_slab):
             rows = pl.ds(t * tile, tile)
             from_sib[q, rows, :] = (block_row(first + t) + from_sib[q, rows, :].astype(F32)).astype(BF16)
-        pltpu.make_async_copy(from_sib.at[q], pair_out.at[q], p_sem.at[q]).start()
+
+        @pl.when(((place != 1) | (q != places - 1)) & ((place != places - 2) | (q != 0)))
+        def _():
+            pltpu.make_async_copy(from_sib.at[q], pair_out.at[q], p_sem.at[q]).start()
+
+    def hop(side, h, q, device):
+        rows = pl.ds(h * half, half)
+        return remote(
+            from_sib.at[q, rows], hop_in.at[side, rows], e_send.at[side, h], e_recv.at[side, h], device
+        )
+
+    for_sibling(0)
+    for_sibling(1)
+    for_self(0)
+    for h in range(HALVES):
+
+        @pl.when(place == 0)
+        def _():
+            hop(0, h, places - 1, right).start()
+
+        @pl.when(place == places - 1)
+        def _():
+            hop(1, h, 0, left).start()
+
+    def both(k, carry):
+        for_sibling(k + 1)
+        for_self(k)
         return carry
 
-    lax.fori_loop(0, places, for_self, 0)
-
+    lax.fori_loop(1, places - 1, both, 0)
+    for_self(places - 1)
+    relay(3)
     for step in range(4, places):
         relay(step)
+
+    def land(side, q, device):
+        for h in range(HALVES):
+            rows = pl.ds(h * half, half)
+            hop(side, h, q, device).wait_recv()
+            from_sib[q, rows, :] = (
+                from_sib[q, rows, :].astype(F32) + hop_in[side, rows, :].astype(F32)
+            ).astype(BF16)
+        pltpu.make_async_copy(from_sib.at[q], pair_out.at[q], p_sem.at[q]).start()
+
+    @pl.when(place == 1)
+    def _():
+        land(0, places - 1, left)
+
+    @pl.when(place == places - 2)
+    def _():
+        land(1, 0, right)
+
+    for h in range(HALVES):
+
+        @pl.when(place == 0)
+        def _():
+            hop(0, h, places - 1, right).wait_send()
+
+        @pl.when(place == places - 1)
+        def _():
+            hop(1, h, 0, left).wait_send()
 
     for q in range(places):
         pltpu.make_async_copy(from_sib.at[q], pair_out.at[q], p_sem.at[q]).wait()
@@ -269,8 +323,8 @@
         held[q, rows, :] = (arrived[q, rows, :].astype(F32) + pair[q, rows, :].astype(F32)).astype(BF16)
 
     def relay(step):
-        to_right = places - 1 + place - step
-        to_left = step - (places - 1) + place
+        to_right = places - 2 + place - step
+        to_left = place + step + 2 - places
         for h in range(HALVES):
             rows = pl.ds(h * half, half)
 
@@ -279,11 +333,13 @@
                 q = to_right
                 target, sems = r_in.at[q, rows], (r_send.at[q, h], r_recv.at[q, h])
 
-                @pl.when(place == 0)
+                first = (place == 0) | ((place == 1) & (q == places - 1))
+
+                @pl.when(first)
                 def _():
                     remote(pair.at[q, rows], target, *sems, right).start()
 
-                @pl.when(place > 0)
+                @pl.when(jnp.logical_not(first))
                 def _():
                     remote(target, target, *sems, left).wait_recv()
                     add(r_sum, r_in, q, rows)
@@ -294,11 +350,13 @@
                 q = to_left
                 target, sems = l_in.at[q, rows], (l_send.at[q, h], l_recv.at[q, h])
 
-                @pl.when(place == places - 1)
+                first = (place == places - 1) | ((place == places - 2) & (q == 0))
+
+                @pl.when(first)
                 def _():
                     remote(pair.at[q, rows], target, *sems, left).start()
 
-                @pl.when(place < places - 1)
+                @pl.when(jnp.logical_not(first))
                 def _():
                     remote(target, target, *sems, right).wait_recv()
                     add(l_sum, l_in, q, rows)
@@ -317,8 +375,7 @@
         send(w_row.at[row], w_row.at[row], b_send.at[d], b_recv.at[d], peer)
     for h in range(1, HALVES):
         send_spread(h)
-    if places > 2:
-        relay(1)
+    relay(1)
     for d in range(1, n_row):
         sender = lax.rem(row - d + n_row, n_row)
         remote(
@@ -330,7 +387,7 @@
             weight_grad.at[piece(rep)], weight_grad.at[piece(rep)], g_send.at[d], g_recv.at[d], peer
         )
 
-    for step in range(2, places - 1):
+    for step in range(2, places - 2):
         relay(step)
     own.wait()
     grad = s_in[row].astype(F32)
@@ -379,11 +436,11 @@
         for h in range(HALVES):
             held = r_sum.at[q, pl.ds(h * half, half)]
 
-            @pl.when(place < q)
+            @pl.when((place < q) & ((place != 0) | (q != places - 1)))
             def _():
                 remote(held, held, r_send.at[q, h], r_recv.at[q, h], right).wait_send()
 
-            @pl.when(place > q)
+            @pl.when((place > q) & ((place != places - 1) | (q != 0)))
             def _():
                 remote(held, held, l_send.at[q, h], l_recv.at[q, h], left).wait_send()
 
@@ -432,6 +489,7 @@
                 pltpu.VMEM((tiles + 1, tile, depth), BF16),
                 pltpu.VMEM((places, slab, depth), BF16),
                 pltpu.VMEM((places, slab, depth), BF16),
+                pltpu.VMEM((2, slab, depth), BF16),
                 dma((5,)),
                 dma((n_row,)), dma((n_row,)),
                 dma((places, HALVES)), dma((places, HALVES)),
@@ -439,6 +497,7 @@
                 dma((places, HALVES)), dma((places, HALVES)),
                 dma((places,)), dma((places,)),
                 dma((places,)),
+                dma((2, HALVES)), dma((2, HALVES)),
             ],
             compiler_params=pltpu.CompilerParams(
                 collective_id=0, has_side_effects=True, vmem_limit_bytes=VMEM_LIMIT

time: 57.3 us -> 55.9 us (0.976)
  local copies, waits for them, and re-layouts: 3.96 us -> 3.13 us
  Pallas kernels: 52.3 us -> 51.7 us
    pallas_call x1, Pallas kernels: 7.84 us -> 6.69 us  [shards(): pl.pallas_call(backward_kernel, name='backward', grid=(tile_rows // chunk...]
    pallas_call x1, Pallas kernels: 25 us -> 26 us  [shards(): pl.pallas_call(functools.partial(forward_kernel, n_row, n_rep), name='for...]
    unnamed x11 -> x13, local copies, waits for them, and re-layouts: 3.96 us -> 3.13 us
where the time goes in v4:
time: 55.9 us; the launch traced here: 55.6 us
  Pallas kernels  51.7 us (92%)
  local copies, waits for them, and re-layouts  3.13 us (6%)
  between operations  0.72 us (1%)
    pallas_call x1, Pallas kernels, shards(): pl.pallas_call(functools.partial(forward_kernel, n_row, n_rep), name='for...  26 us
    pallas_call x1, Pallas kernels, shards(): pl.pallas_call(functools.partial(reduce_kernel, n_row, n_rep, 1.0 / math....  19.1 us
    pallas_call x1, Pallas kernels, shards(): pl.pallas_call(backward_kernel, name='backward', grid=(tile_rows // chunk...  6.69 us
    unnamed x13, local copies, waits for them, and re-layouts  3.13 us

profile of v4, /device:TPU:0, one launch (start us, length us, event | category | flops | bytes accessed | tf_op | source)
XLA Modules:
  0.0 55.6 jit_solution(9731893896187735244)
XLA Ops:
  0.6 0.0 copy-start.4
  0.6 0.0 copy-start.3
  0.7 0.0 copy-start.2
  0.7 26.0 %forward.1 = (bf16[4,768,128]{2,1,0:T(8,128)(2,1)}, bf16[8,768,128]{2,1,0:T(8,128)(2,1)}, bf16[4,768,128]{2,1,0:T(8,128)(2,1)}) custom-call(bf16[768,128]{1,0:T(8,128)(2,1)} %feat_hbm.1, s32[1,768]{1,0:T(1,128)} %order_hbm.1, bf16[128,128]{1,0:T(8,128)(2,1)} %weight.1, s32[1,4,48]{2,1,0:T(4,128)} %bitcast.8, s32[1,48]{1,0:T(1,128)} %bitcast.10, ...), custom_call_target="tpu_custom_call" | custom-call | tf_op jit(solution)/shard_map/forward/pallas_call | solution.py:474
  26.6 0.0 copy-done.4
  26.6 0.0 copy-done.3
  26.6 0.0 copy-start
  26.7 1.1 %copy-done = bf16[4,768,128]{2,1,0:T(8,128)(2,1)S(1)} copy-done((bf16[4,768,128]{2,1,0:T(8,128)(2,1)S(1)}, bf16[4,768,128]{2,1,0:T(8,128)(2,1)}, u32[]{:S(2)}) %copy-start) | copy-done | bytes 786456
  27.8 0.0 copy-start.1
  27.8 6.7 %backward.1 = (bf16[3072,128]{1,0:T(8,128)(2,1)S(1)}, f32[128,128]{1,0:T(8,128)S(1)}) custom-call(s32[1,4,48]{2,1,0:T(4,128)S(1)} %bitcast.9, s32[1,48]{1,0:T(1,128)S(1)} %bitcast.11, bf16[48,4,128,128]{3,2,1,0:T(8,128)(2,1)} %bitcast.13, bf16[48,128,128]{2,1,0:T(8,128)(2,1)} %bitcast.14, bf16[3072,128]{1,0:T(8,128)(2,1)S(1)} %bitcast.6), custom_call_target="tpu_custom_call" | custom-call | tf_op jit(solution)/shard_map/backward/pallas_call | solution.py:508
  34.5 0.0 copy-done.2
  34.5 0.0 copy-done.1
  34.5 19.1 %reduce.1 = (bf16[768,128]{1,0:T(8,128)(2,1)S(1)}, bf16[768,128]{1,0:T(8,128)(2,1)S(1)}, f32[128,128]{1,0:T(8,128)S(1)}) custom-call(bf16[4,768,128]{2,1,0:T(8,128)(2,1)S(1)} %copy-done.1, bf16[4,768,128]{2,1,0:T(8,128)(2,1)S(1)} %bitcast.7, f32[128,128]{1,0:T(8,128)S(1)} %get-tuple-element.12.local, bf16[128,128]{1,0:T(8,128)(2,1)S(1)} %copy-done.2), custom_call_target="tpu_custom_call" | custom-call | tf_op jit(solution)/shard_map/reduce/pallas_call | solution.py:532
  53.6 0.7 %copy.13 = bf16[768,128]{1,0:T(8,128)(2,1)} copy(bf16[768,128]{1,0:T(8,128)(2,1)S(1)} %get-tuple-element.16) | data formatting | bytes 393216
  54.3 0.7 %copy.14 = bf16[768,128]{1,0:T(8,128)(2,1)} copy(bf16[768,128]{1,0:T(8,128)(2,1)S(1)} %get-tuple-element.17) | data formatting | bytes 393216
  54.9 0.6 %copy.15 = f32[128,128]{1,0:T(8,128)} copy(f32[128,128]{1,0:T(8,128)S(1)} %get-tuple-element.18) | data formatting | bytes 131072
Async XLA Ops:
  0.6 26.0 %copy-start.4 = (s32[48,1]{0,1:T(1,128)S(1)}, s32[48,1]{0,1:T(1,128)}, u32[]{:S(2)}) copy-start(s32[48,1]{0,1:T(1,128)} %param.12) | copy-start | bytes 580
  0.6 26.0 %copy-start.3 = (s32[48,1,4]{0,2,1:T(4,128)S(1)}, s32[48,1,4]{0,2,1:T(4,128)}, u32[]{:S(2)}) copy-start(s32[48,1,4]{0,2,1:T(4,128)} %param.11) | copy-start | bytes 2308
  0.7 33.8 %copy-start.2 = (bf16[128,128]{1,0:T(8,128)(2,1)S(1)}, bf16[128,128]{1,0:T(8,128)(2,1)}, u32[]{:S(2)}) copy-start(bf16[128,128]{1,0:T(8,128)(2,1)} %weight.1) | copy-start | bytes 98308
  26.6 1.1 %copy-start = (bf16[4,768,128]{2,1,0:T(8,128)(2,1)S(1)}, bf16[4,768,128]{2,1,0:T(8,128)(2,1)}, u32[]{:S(2)}) copy-start(bf16[4,768,128]{2,1,0:T(8,128)(2,1)} %get-tuple-element.10) | copy-start | bytes 2359300
  27.8 6.7 %copy-start.1 = (bf16[4,768,128]{2,1,0:T(8,128)(2,1)S(1)}, bf16[4,768,128]{2,1,0:T(8,128)(2,1)}, u32[]{:S(2)}) copy-start(bf16[4,768,128]{2,1,0:T(8,128)(2,1)} %get-tuple-element.8.pair_hbm) | copy-start | bytes 2359300

commit v5 on v4

--- a/solution.py
+++ b/solution.py
@@ -12,7 +12,7 @@
 VMEM_LIMIT = 63 * 1024 * 1024
 F32 = jnp.float32
 BF16 = jnp.bfloat16
-MIDDLE_LIMIT = 52 * 1024 * 1024
+MIDDLE_LIMIT = 53 * 1024 * 1024
 LATER_LIMIT = 40 * 1024 * 1024
 HALVES = 2
 
@@ -504,7 +504,7 @@
             ),
         )(features, node_order, weight, cols, counts, cotangent, vals)
 
-        chunk = 8
+        chunk = 16
         spread, local = pl.pallas_call(
             backward_kernel,
             name="backward",

time: 55.9 us -> 54.4 us (0.973)
  local copies, waits for them, and re-layouts: 3.13 us -> 2 us
    unnamed x13 -> x11, local copies, waits for them, and re-layouts: 3.13 us -> 2 us
where the time goes in v5:
time: 54.4 us; the launch traced here: 54.2 us
  Pallas kernels  51.5 us (95%)
  local copies, waits for them, and re-layouts  2 us (4%)
  between operations  0.72 us (1%)
    pallas_call x1, Pallas kernels, shards(): pl.pallas_call(functools.partial(forward_kernel, n_row, n_rep), name='for...  26 us
    pallas_call x1, Pallas kernels, shards(): pl.pallas_call(functools.partial(reduce_kernel, n_row, n_rep, 1.0 / math....  19.1 us
    pallas_call x1, Pallas kernels, shards(): pl.pallas_call(backward_kernel, name='backward', grid=(tile_rows // chunk...  6.48 us
    unnamed x11, local copies, waits for them, and re-layouts  2 us

profile of v5, /device:TPU:0, one launch (start us, length us, event | category | flops | bytes accessed | tf_op | source)
XLA Modules:
  0.0 54.2 jit_solution(14866697456330309879)
XLA Ops:
  0.6 0.0 copy-start.3
  0.6 0.0 copy-start.2
  0.7 0.0 copy-start.1
  0.7 26.0 %forward.1 = (bf16[4,768,128]{2,1,0:T(8,128)(2,1)}, bf16[8,768,128]{2,1,0:T(8,128)(2,1)}, bf16[4,768,128]{2,1,0:T(8,128)(2,1)}) custom-call(bf16[768,128]{1,0:T(8,128)(2,1)} %feat_hbm.1, s32[1,768]{1,0:T(1,128)} %order_hbm.1, bf16[128,128]{1,0:T(8,128)(2,1)} %weight.1, s32[1,4,48]{2,1,0:T(4,128)} %bitcast.7, s32[1,48]{1,0:T(1,128)} %bitcast.9, ...), custom_call_target="tpu_custom_call" | custom-call | tf_op jit(solution)/shard_map/forward/pallas_call | solution.py:474
  26.6 0.0 copy-start
  26.6 0.0 copy-done.3
  26.7 0.0 copy-done.2
  26.7 6.5 %backward.1 = (bf16[3072,128]{1,0:T(8,128)(2,1)S(1)}, f32[128,128]{1,0:T(8,128)S(1)}) custom-call(s32[1,4,48]{2,1,0:T(4,128)S(1)} %bitcast.8, s32[1,48]{1,0:T(1,128)S(1)} %bitcast.10, bf16[48,4,128,128]{3,2,1,0:T(8,128)(2,1)} %bitcast.12, bf16[48,128,128]{2,1,0:T(8,128)(2,1)} %bitcast.13, bf16[3072,128]{1,0:T(8,128)(2,1)} %bitcast.14), custom_call_target="tpu_custom_call" | custom-call | tf_op jit(solution)/shard_map/backward/pallas_call | solution.py:508
  33.1 0.0 copy-done.1
  33.2 0.0 copy-done
  33.2 19.1 %reduce.1 = (bf16[768,128]{1,0:T(8,128)(2,1)S(1)}, bf16[768,128]{1,0:T(8,128)(2,1)S(1)}, f32[128,128]{1,0:T(8,128)S(1)}) custom-call(bf16[4,768,128]{2,1,0:T(8,128)(2,1)S(1)} %copy-done, bf16[4,768,128]{2,1,0:T(8,128)(2,1)S(1)} %bitcast.6, f32[128,128]{1,0:T(8,128)S(1)} %get-tuple-element.12.local, bf16[128,128]{1,0:T(8,128)(2,1)S(1)} %copy-done.1), custom_call_target="tpu_custom_call" | custom-call | tf_op jit(solution)/shard_map/reduce/pallas_call | solution.py:532
  52.2 0.7 %copy.13 = bf16[768,128]{1,0:T(8,128)(2,1)} copy(bf16[768,128]{1,0:T(8,128)(2,1)S(1)} %get-tuple-element.16) | data formatting | bytes 393216
  52.9 0.7 %copy.14 = bf16[768,128]{1,0:T(8,128)(2,1)} copy(bf16[768,128]{1,0:T(8,128)(2,1)S(1)} %get-tuple-element.17) | data formatting | bytes 393216
  53.6 0.6 %copy.15 = f32[128,128]{1,0:T(8,128)} copy(f32[128,128]{1,0:T(8,128)S(1)} %get-tuple-element.18) | data formatting | bytes 131072
Async XLA Ops:
  0.6 26.0 %copy-start.3 = (s32[48,1]{0,1:T(1,128)S(1)}, s32[48,1]{0,1:T(1,128)}, u32[]{:S(2)}) copy-start(s32[48,1]{0,1:T(1,128)} %param.12) | copy-start | bytes 580
  0.6 26.0 %copy-start.2 = (s32[48,1,4]{0,2,1:T(4,128)S(1)}, s32[48,1,4]{0,2,1:T(4,128)}, u32[]{:S(2)}) copy-start(s32[48,1,4]{0,2,1:T(4,128)} %param.11) | copy-start | bytes 2308
  0.7 32.5 %copy-start.1 = (bf16[128,128]{1,0:T(8,128)(2,1)S(1)}, bf16[128,128]{1,0:T(8,128)(2,1)}, u32[]{:S(2)}) copy-start(bf16[128,128]{1,0:T(8,128)(2,1)} %weight.1) | copy-start | bytes 98308
  26.6 6.5 %copy-start = (bf16[4,768,128]{2,1,0:T(8,128)(2,1)S(1)}, bf16[4,768,128]{2,1,0:T(8,128)(2,1)}, u32[]{:S(2)}) copy-start(bf16[4,768,128]{2,1,0:T(8,128)(2,1)} %get-tuple-element.8.pair_hbm) | copy-start | bytes 2359300

commit v6 on v5

--- a/solution.py
+++ b/solution.py
@@ -504,7 +504,7 @@
             ),
         )(features, node_order, weight, cols, counts, cotangent, vals)
 
-        chunk = 16
+        chunk = 24
         spread, local = pl.pallas_call(
             backward_kernel,
             name="backward",

time: 54.4 us -> 53.1 us (0.976)
  Pallas kernels: 51.5 us -> 50.2 us
    pallas_call x1, Pallas kernels: 6.48 us -> 5.17 us  [shards(): pl.pallas_call(backward_kernel, name='backward', grid=(tile_rows // chunk...]
where the time goes in v6:
time: 53.1 us; the launch traced here: 52.9 us
  Pallas kernels  50.2 us (95%)
  local copies, waits for them, and re-layouts  2 us (4%)
  between operations  0.72 us (1%)
    pallas_call x1, Pallas kernels, shards(): pl.pallas_call(functools.partial(forward_kernel, n_row, n_rep), name='for...  26 us
    pallas_call x1, Pallas kernels, shards(): pl.pallas_call(functools.partial(reduce_kernel, n_row, n_rep, 1.0 / math....  19.1 us
    pallas_call x1, Pallas kernels, shards(): pl.pallas_call(backward_kernel, name='backward', grid=(tile_rows // chunk...  5.17 us
    unnamed x11, local copies, waits for them, and re-layouts  2 us

profile of v6, /device:TPU:0, one launch (start us, length us, event | category | flops | bytes accessed | tf_op | source)
XLA Modules:
  0.0 52.9 jit_solution(2531123764764908429)
XLA Ops:
  0.6 0.0 copy-start.3
  0.6 0.0 copy-start.2
  0.7 0.0 copy-start.1
  0.7 26.0 %forward.1 = (bf16[4,768,128]{2,1,0:T(8,128)(2,1)}, bf16[8,768,128]{2,1,0:T(8,128)(2,1)}, bf16[4,768,128]{2,1,0:T(8,128)(2,1)}) custom-call(bf16[768,128]{1,0:T(8,128)(2,1)} %feat_hbm.1, s32[1,768]{1,0:T(1,128)} %order_hbm.1, bf16[128,128]{1,0:T(8,128)(2,1)} %weight.1, s32[1,4,48]{2,1,0:T(4,128)} %bitcast.7, s32[1,48]{1,0:T(1,128)} %bitcast.9, ...), custom_call_target="tpu_custom_call" | custom-call | tf_op jit(solution)/shard_map/forward/pallas_call | solution.py:474
  26.6 0.0 copy-start
  26.6 0.0 copy-done.3
  26.7 0.0 copy-done.2
  26.7 5.2 %backward.1 = (bf16[3072,128]{1,0:T(8,128)(2,1)S(1)}, f32[128,128]{1,0:T(8,128)S(1)}) custom-call(s32[1,4,48]{2,1,0:T(4,128)S(1)} %bitcast.8, s32[1,48]{1,0:T(1,128)S(1)} %bitcast.10, bf16[48,4,128,128]{3,2,1,0:T(8,128)(2,1)} %bitcast.12, bf16[48,128,128]{2,1,0:T(8,128)(2,1)} %bitcast.13, bf16[3072,128]{1,0:T(8,128)(2,1)} %bitcast.14), custom_call_target="tpu_custom_call" | custom-call | tf_op jit(solution)/shard_map/backward/pallas_call | solution.py:508
  31.8 0.0 copy-done.1
  31.9 0.0 copy-done
  31.9 19.1 %reduce.1 = (bf16[768,128]{1,0:T(8,128)(2,1)S(1)}, bf16[768,128]{1,0:T(8,128)(2,1)S(1)}, f32[128,128]{1,0:T(8,128)S(1)}) custom-call(bf16[4,768,128]{2,1,0:T(8,128)(2,1)S(1)} %copy-done, bf16[4,768,128]{2,1,0:T(8,128)(2,1)S(1)} %bitcast.6, f32[128,128]{1,0:T(8,128)S(1)} %get-tuple-element.12.local, bf16[128,128]{1,0:T(8,128)(2,1)S(1)} %copy-done.1), custom_call_target="tpu_custom_call" | custom-call | tf_op jit(solution)/shard_map/reduce/pallas_call | solution.py:532
  51.0 0.7 %copy.13 = bf16[768,128]{1,0:T(8,128)(2,1)} copy(bf16[768,128]{1,0:T(8,128)(2,1)S(1)} %get-tuple-element.16) | data formatting | bytes 393216
  51.6 0.7 %copy.14 = bf16[768,128]{1,0:T(8,128)(2,1)} copy(bf16[768,128]{1,0:T(8,128)(2,1)S(1)} %get-tuple-element.17) | data formatting | bytes 393216
  52.3 0.6 %copy.15 = f32[128,128]{1,0:T(8,128)} copy(f32[128,128]{1,0:T(8,128)S(1)} %get-tuple-element.18) | data formatting | bytes 131072
Async XLA Ops:
  0.6 26.0 %copy-start.3 = (s32[48,1]{0,1:T(1,128)S(1)}, s32[48,1]{0,1:T(1,128)}, u32[]{:S(2)}) copy-start(s32[48,1]{0,1:T(1,128)} %param.12) | copy-start | bytes 580
  0.6 26.0 %copy-start.2 = (s32[48,1,4]{0,2,1:T(4,128)S(1)}, s32[48,1,4]{0,2,1:T(4,128)}, u32[]{:S(2)}) copy-start(s32[48,1,4]{0,2,1:T(4,128)} %param.11) | copy-start | bytes 2308
  0.7 31.2 %copy-start.1 = (bf16[128,128]{1,0:T(8,128)(2,1)S(1)}, bf16[128,128]{1,0:T(8,128)(2,1)}, u32[]{:S(2)}) copy-start(bf16[128,128]{1,0:T(8,128)(2,1)} %weight.1) | copy-start | bytes 98308
  26.6 5.2 %copy-start = (bf16[4,768,128]{2,1,0:T(8,128)(2,1)S(1)}, bf16[4,768,128]{2,1,0:T(8,128)(2,1)}, u32[]{:S(2)}) copy-start(bf16[4,768,128]{2,1,0:T(8,128)(2,1)} %get-tuple-element.8.pair_hbm) | copy-start | bytes 2359300
